TPU v7x, 768 devices: a whole 4x8x12 slice. The times are simulated.
768 devices in a mesh: vert: 24 (over z, core), feat: 32 (over y, x).
Axes of the slice: x: 4, y: 8, z: 12, core: 2. Of those that a mesh axis runs over, the one named last changes fastest.
Arguments:
- node_feats: bfloat16 [128, 196608], P('feat', 'vert'), may hold values from -6 to 6
- w_self: bfloat16 [128, 256], replicated, may hold values from -0.5 to 0.5
- w_neigh: bfloat16 [128, 256], replicated, may hold values from -6 to 6
- out_bias: float32 [256], replicated, may hold values from -3 to 3
- adjacency: bfloat16 [73728, 128, 128], P(('vert', 'feat')), may hold values from 0.0099487305 to 1
- block_dst: int32 [73728], P(('vert', 'feat')), may hold values from 0 to 1, as said below
- block_src: int32 [73728], P(('vert', 'feat')), may hold values from 0 to 111, as said below
- block_count: int32 [768], P(('vert', 'feat')), may hold values from 49 to 96, as said below
- send_list: int32 [24, 24, 2], P('vert'), may hold values from 0 to 63, as said below
- grad_out: bfloat16 [196608, 256], P(('vert', 'feat')), may hold values from -6 to 6
Outputs:
- activated: bfloat16 [196608, 256], P(('vert', 'feat'))
- grad_feats: float32 [128, 196608], P('feat', 'vert')
- grad_self: float32 [128, 256], replicated
- grad_neigh: float32 [128, 256], replicated
- grad_bias: float32 [256], replicated
Inputs may be any that keep to these rules, and one draw needn't show every extreme that they name: `block_count`: some device has exactly 96 live blocks; blocks past a device's count are padding. `block_dst`: the first 2 blocks of every device have destination t, t = 0 to 1. `block_src`: the first 2 blocks of member m have source m * 2 + t. Below 64: a tile of the own slab; else 64 + p * 2 + s, slot s of what slab p sends, with p never the own slab. `send_list`: entry [p, r, s] is a tile of slab p, counted within slab p.
All inputs are finite; a program needn't handle non-finite values.
Results may differ from a plain program's by a relative error of at most 0.015.
Values may be sent and summed in bfloat16 or wider, within the bound.
No kernel may reach another device: no remote copies, remote signals or barrier semaphores. Data moves between devices by JAX's collectives and lax.ppermute only.
A program may use at most 32 MiB of HBM per device.

v0:
```python
import jax
import jax.numpy as jnp
from jax import lax
from jax.sharding import PartitionSpec as P


def block_weights(adjacency, block_dst, live_count, tile_count):
    blocks = adjacency.shape[0]
    living = (jnp.arange(blocks) < live_count).astype(jnp.float32)
    placing = (block_dst[:, None] == jnp.arange(tile_count)[None, :]).astype(jnp.float32) * living[
        :, None
    ]
    ones_col = jnp.ones((adjacency.shape[2],), jnp.bfloat16)
    row_sums = jnp.einsum("bik,k->bi", adjacency, ones_col, preferred_element_type=jnp.float32)
    degree = jnp.einsum("bt,bi->ti", placing, row_sums, precision=lax.Precision.HIGHEST)
    return (living, placing, degree)


def gather_sum(src_table, adjacency, block_src, placing):
    sources = jnp.take(src_table, block_src, axis=1)
    contrib = jnp.einsum("bik,cbk->cbi", adjacency, sources, preferred_element_type=jnp.float32)
    return jnp.einsum("bt,cbi->cti", placing, contrib, precision=lax.Precision.HIGHEST)


def local(
    node_feats,
    w_self,
    w_neigh,
    out_bias,
    adjacency,
    block_dst,
    block_src,
    block_count,
    send_list,
    grad_out,
):
    feat_local, slab_rows = node_feats.shape
    tile_size = adjacency.shape[1]
    tile_count = slab_rows // tile_size
    slab_count = send_list.shape[1]
    slot_count = send_list.shape[2]
    owned_rows = grad_out.shape[0]
    dev_tiles = owned_rows // tile_size
    first_tile = lax.axis_index("feat") * dev_tiles
    table_tiles = tile_count + slab_count * slot_count
    tile_view = node_feats.reshape(feat_local, tile_count, tile_size)
    send_flat = send_list[0].reshape(-1)
    living, placing, degree = block_weights(adjacency, block_dst, block_count[0], dev_tiles)
    outgoing = jnp.take(tile_view, send_flat, axis=1).reshape(
        feat_local, slab_count, slot_count, tile_size
    )
    incoming = lax.all_to_all(outgoing, "vert", split_axis=1, concat_axis=1, tiled=True)
    src_table = jnp.concatenate(
        [tile_view, incoming.reshape(feat_local, slab_count * slot_count, tile_size)], axis=1
    )
    rows_in = lax.all_gather(src_table, "feat", axis=0, tiled=True)
    own_part = lax.dynamic_slice_in_dim(rows_in, first_tile, dev_tiles, 1).astype(jnp.float32)
    gathered = jnp.concatenate(
        [gather_sum(rows_in, adjacency, block_src, placing), own_part], axis=1
    )
    summed = gathered[:, :dev_tiles]
    own_feats = gathered[:, dev_tiles:].astype(jnp.bfloat16)
    feat_count = summed.shape[0]
    neigh_mean = (summed / degree[None]).astype(jnp.bfloat16).reshape(feat_count, owned_rows)
    own_feats = own_feats.reshape(feat_count, owned_rows)
    contract_first = (((0,), (0,)), ((), ()))
    preact = (
        lax.dot_general(own_feats, w_self, contract_first, preferred_element_type=jnp.float32)
        + lax.dot_general(neigh_mean, w_neigh, contract_first, preferred_element_type=jnp.float32)
        + out_bias
    )
    activated = jax.nn.silu(preact).astype(jnp.bfloat16)
    sigmoid_pre = jax.nn.sigmoid(preact)
    grad_pre = (
        grad_out.astype(jnp.float32) * sigmoid_pre * (1.0 + preact * (1.0 - sigmoid_pre))
    ).astype(jnp.bfloat16)
    part_self = jnp.dot(own_feats, grad_pre, preferred_element_type=jnp.float32)
    part_neigh = jnp.dot(neigh_mean, grad_pre, preferred_element_type=jnp.float32)
    ones_row = jnp.ones((owned_rows,), jnp.bfloat16)
    part_bias = jnp.dot(ones_row, grad_pre, preferred_element_type=jnp.float32)
    grad_self, grad_neigh, grad_bias = lax.psum(
        (part_self, part_neigh, part_bias), ("vert", "feat")
    )
    contract_last = (((1,), (1,)), ((), ()))
    from_self = lax.dot_general(w_self, grad_pre, contract_last, preferred_element_type=jnp.float32)
    from_mean = lax.dot_general(
        w_neigh, grad_pre, contract_last, preferred_element_type=jnp.float32
    )
    self_tiles = from_self.reshape(feat_count, dev_tiles, tile_size)
    grad_mean = (from_mean.reshape(feat_count, dev_tiles, tile_size) / degree[None]).astype(
        jnp.bfloat16
    )
    src_onehot = (block_src[:, None] == jnp.arange(table_tiles)[None, :]).astype(jnp.float32)
    at_dst = jnp.take(grad_mean, block_dst, axis=1)
    backward = jnp.einsum("bik,cbi->cbk", adjacency, at_dst, preferred_element_type=jnp.float32)
    backward = backward * living[None, :, None]
    dev_terms = jnp.einsum("bn,cbk->cnk", src_onehot, backward, precision=lax.Precision.HIGHEST)
    placed = lax.dynamic_slice_in_dim(dev_terms, first_tile, dev_tiles, 1) + self_tiles
    slab_terms = lax.psum_scatter(
        lax.dynamic_update_slice_in_dim(dev_terms, placed, first_tile, 1).astype(jnp.bfloat16),
        "feat",
        scatter_dimension=0,
        tiled=True,
    ).astype(jnp.float32)
    away = slab_terms[:, tile_count:].reshape(feat_local, slab_count, slot_count, tile_size)
    returned = lax.all_to_all(
        away.astype(jnp.bfloat16), "vert", split_axis=1, concat_axis=1, tiled=True
    ).astype(away.dtype)
    landing = (send_flat[:, None] == jnp.arange(tile_count)[None, :]).astype(jnp.float32)
    landed = jnp.einsum(
        "st,csk->ctk",
        landing,
        returned.reshape(feat_local, slab_count * slot_count, tile_size),
        precision=lax.Precision.HIGHEST,
    )
    grad_feats = (slab_terms[:, :tile_count] + landed).reshape(feat_local, slab_rows)
    return (activated, grad_feats, grad_self, grad_neigh, grad_bias)


def solution(mesh):
    in_specs = (
        P("feat", "vert"),
        P(),
        P(),
        P(),
        P(("vert", "feat"), None, None),
        P(("vert", "feat")),
        P(("vert", "feat")),
        P(("vert", "feat")),
        P("vert", None, None),
        P(("vert", "feat"), None),
    )
    out_specs = (P(("vert", "feat"), None), P("feat", "vert"), P(), P(), P())
    return jax.shard_map(local, mesh=mesh, in_specs=in_specs, out_specs=out_specs, check_vma=False)
```

profile of v0, /device:TPU:1, one launch (start us, length us, event | category | flops | bytes accessed | tf_op | source)
XLA Modules:
  0.0 879.0 jit_solution(9402306532538105276)
XLA Ops:
  7.2 0.8 compare_and_fusion.2
  8.1 0.8 copy.36
  9.1 1.5 gather_fusion
  10.7 26.6 %all_to_all.10 = bf16[4,24,2,128]{3,0,2,1:T(4,128)(2,1)S(1)} all-to-all(bf16[4,24,2,128]{3,0,2,1:T(4,128)(2,1)S(1)} %broadcast_select_fusion), channel_id=1, replica_groups=mesh['vert'=24,'feat'=32] {'vert'}, dimensions={1} | all-to-all | bytes 98304 | tf_op jit(solution)/shard_map/all_to_all | solution.py:52
  37.3 0.9 pad_maximum_fusion
  42.2 1.2 compare_and_fusion
  43.4 0.9 fusion.54
  44.5 77.2 %all-gather.2.cloned.1.call-done = bf16[128,112,128]{2,1,0:T(8,128)(2,1)} async-done(((bf16[4,112,128]{2,1,0:T(8,128)(2,1)}), bf16[128,112,128]{2,1,0:T(8,128)(2,1)}) %all-gather.2.cloned.1.call-update) | async-done | bytes 3670032 | tf_op jit(solution)/shard_map/all_gather | solution.py:56
  121.7 1.0 constant_dynamic-slice_fusion
  122.9 4.9 copy.39
  127.7 4.8 gather_fusion.1
  132.7 4.2 fusion.12
  137.0 6.9 fusion.28
  143.9 1.0 multiply_convert_fusion
  144.8 0.8 fusion.64
  145.7 0.8 fusion.63
  146.5 1.0 copy.49
  147.6 1.0 copy.50
  148.7 3.1 gather_fusion.2
  151.8 3.0 multiply_bitcast_fusion
  154.8 7.3 fusion
  162.7 2.3 convert_element_type.46
  165.8 0.8 fusion.32
  166.6 0.9 fusion.65
  167.5 223.8 %reduce-scatter.2.cloned.1.call-done = bf16[4,112,128]{2,1,0:T(8,128)(2,1)} async-done(((bf16[128,112,128]{2,1,0:T(8,128)(2,1)}), bf16[4,112,128]{2,1,0:T(8,128)(2,1)}) %reduce-scatter.2.cloned.1.call-update) | async-done | bytes 114704 | tf_op jit(solution)/shard_map/reduce_scatter | solution.py:99
  391.3 0.8 slice.20
  392.8 15.2 %all-to-all-start.1 = ((bf16[4,24,2,128]{3,2,0,1:T(2,128)(2,1)}), bf16[4,24,2,128]{3,2,0,1:T(2,128)(2,1)S(1)}, u32[]{:S(2)}, u32[]{:S(2)}) async-start(bf16[4,24,2,128]{3,2,0,1:T(2,128)(2,1)} %copy.45), calls=%async_computation.2 | async-start | bytes 98304 | tf_op jit(solution)/shard_map/all_to_all | solution.py:106
  408.2 109.0 %psum.23 = f32[256]{0:T(256)} all-reduce(f32[256]{0:T(256)S(1)} %bitcast.107), channel_id=1, replica_groups=mesh['vert'=24,'feat'=32] {'vert','feat'}, use_global_device_ids=true, to_apply=%region_3.4 | all-reduce | flops 256 | bytes 2048 | tf_op jit(solution)/shard_map/psum | solution.py:81
  517.2 1.1 fusion.21
  519.0 350.3 %all-reduce.3.cloned.1.call-done = (f32[128,256]{1,0:T(8,128)}, f32[128,256]{1,0:T(8,128)}) async-done(((f32[128,256]{1,0:T(8,128)}, f32[128,256]{1,0:T(8,128)}), (f32[128,256]{1,0:T(8,128)}, f32[128,256]{1,0:T(8,128)})) %all-reduce.3.cloned.1.call-update) | async-done | bytes 262160 | tf_op jit(solution)/shard_map/psum | solution.py:81
  869.3 1.6 copy.80
  870.9 1.6 copy.81
  (53 shorter events, 7.2 us)
Async XLA Ops:
  7.2 36.3 %copy-start = (bf16[96,128,128]{2,1,0:T(8,128)(2,1)S(1)}, bf16[96,128,128]{2,1,0:T(8,128)(2,1)}, u32[]{:S(2)}) copy-start(bf16[96,128,128]{2,1,0:T(8,128)(2,1)} %param.14) | copy-start | bytes 9437188
  7.2 37.1 %copy-start.7 = (s32[96]{0:T(128)S(1)}, s32[96]{0:T(128)}, u32[]{:S(2)}) copy-start(s32[96]{0:T(128)} %param.15) | copy-start | bytes 1156
  7.2 114.5 %all-gather.2.cloned.1.call-start = ((), (), s32[]{:S(2)}) async-start(), calls=%async_computation.3 | async-start | bytes 3784704 | tf_op jit(solution)/shard_map/all_gather | solution.py:56
  38.9 352.4 %reduce-scatter.2.cloned.1.call-start = ((), (), s32[]{:S(2)}) async-start(), calls=%async_computation.4 | async-start | bytes 3784704 | tf_op jit(solution)/shard_map/reduce_scatter | solution.py:99
  39.6 97.3 %copy-start.5 = (f32[96]{0:T(128)}, f32[96]{0:T(128)S(1)}, u32[]{:S(2)}) copy-start(f32[96]{0:T(128)S(1)} %compare_convert_fusion) | copy-start | bytes 1156
  127.7 4.8 copy-start.3
  136.9 6.9 copy-start.4
  136.9 6.9 copy-start.9
  136.9 6.9 copy-start.10
  143.8 2.7 copy-start.1
  148.6 3.2 copy-start.6
  151.8 3.0 copy-start.8
  164.9 0.8 copy-start.2
  165.0 704.3 %all-reduce.3.cloned.1.call-start = ((), (), s32[]{:S(2)}) async-start(), calls=%async_computation.5 | async-start | bytes 524288 | tf_op jit(solution)/shard_map/psum | solution.py:81
  392.8 124.4 %all-to-all-start.1 = ((bf16[4,24,2,128]{3,2,0,1:T(2,128)(2,1)}), bf16[4,24,2,128]{3,2,0,1:T(2,128)(2,1)S(1)}, u32[]{:S(2)}, u32[]{:S(2)}) async-start(bf16[4,24,2,128]{3,2,0,1:T(2,128)(2,1)} %copy.45), calls=%async_computation.2 | async-start | bytes 98304 | tf_op jit(solution)/shard_map/all_to_all | solution.py:106
Sparse Core Ops, SparseCore 0:
  39.0 82.6 all-gather.1
  165.1 226.1 reduce-scatter.1
  398.6 470.6 all-reduce.2
where the time goes:
time: 880 us; the launch traced here: 879 us
  waiting for transfers between devices  651 us (74%)
  blocking collectives  136 us (15%)
  matrix products  28.1 us (3%)
  local copies, waits for them, and re-layouts  25.8 us (3%)
  starting transfers between devices  15.4 us (2%)
  between operations  14.7 us (2%)
    psum x1, waiting for transfers between devices, local(): lax.psum((part_self, part_neigh, part_bias), ('vert', 'feat'))  350 us
    reduce_scatter x1, waiting for transfers between devices, local(): lax.psum_scatter(lax.dynamic_update_slice_in_dim(dev_terms, placed, first...  224 us
    psum x1, blocking collectives, local(): lax.psum((part_self, part_neigh, part_bias), ('vert', 'feat'))  109 us
    all_gather x1, waiting for transfers between devices, local(): rows_in = lax.all_gather(src_table, 'feat', axis=0, tiled=True)  77.2 us
    all_to_all x1, blocking collectives, local(): lax.all_to_all(outgoing, 'vert', split_axis=1, concat_axis=1, tiled=True)  26.6 us
  transfers between devices with their start and end apart: 4, of which 3 were waited for; matrix products, arithmetic and copies ran while one was open for 1% of the time, Pallas kernels for 0%

commit v1 on v0

v1 whole, which is shorter than its diff:
```python
import functools

import jax
import jax.numpy as jnp
from jax import lax
from jax.experimental import pallas as pl
from jax.experimental.pallas import tpu as pltpu
from jax.sharding import Mesh
from jax.sharding import PartitionSpec as P

X, Y, Z, C = 4, 8, 12, 2
MEMBERS = X * Y
SLABS = Z * C
F = 128
H = 256
TILE = 128
SLOTS = 2
OWN = 64
AWAY = SLABS * SLOTS
TABLE = OWN + AWAY
ROWS = F // MEMBERS
BPD = 96
OWNED = 2 * TILE
GRADS = 5
WIDE = GRADS * TILE
COLS = TABLE * TILE
FULL = COLS + 2 * WIDE
GROUP = 8

BF = jnp.bfloat16
F32 = jnp.float32
VMEM = pl.BlockSpec(memory_space=pltpu.VMEM)
SMEM = pl.BlockSpec(memory_space=pltpu.SMEM)
LIMIT = 40 * 1024 * 1024


def call(body, ins, outs, scratch=()):
    return pl.pallas_call(
        body,
        in_specs=ins,
        out_specs=jax.tree.map(lambda _: VMEM, outs),
        out_shape=outs,
        scratch_shapes=scratch,
        compiler_params=pltpu.CompilerParams(vmem_limit_bytes=LIMIT),
    )


def struct(shape, dtype):
    return jax.ShapeDtypeStruct(shape, dtype)


def lanes(at):
    return pl.ds(pl.multiple_of(at * TILE, TILE), TILE)


def pick_kernel(send, feats, out):
    for slab in range(SLABS):
        for slot in range(SLOTS):
            tile = feats[:, lanes(send[slab * SLOTS + slot])]
            out[slab, slot * ROWS : (slot + 1) * ROWS, :] = tile


def table_kernel(feats, incoming, out):
    out[:, : OWN * TILE] = feats[...]
    for slab in range(SLABS):
        for slot in range(SLOTS):
            at = (OWN + slab * SLOTS + slot) * TILE
            out[:, at : at + TILE] = incoming[slab, slot * ROWS : (slot + 1) * ROWS, :]


def dot(a, b, ca, cb):
    return lax.dot_general(a, b, (((ca,), (cb,)), ((), ())), preferred_element_type=F32)


def split(value):
    high = value.astype(BF)
    return high, (value - high.astype(F32)).astype(BF)


def iota(shape, axis):
    return lax.broadcasted_iota(jnp.int32, shape, axis)


def layer_kernel(
    src, dst, count, first, table, adj, w_self, w_neigh, bias, grad_out, act, out, gathered, terms
):
    live = count[0]
    groups = lax.div(live + (GROUP - 1), GROUP)
    gathered[...] = jnp.zeros_like(gathered)
    ones = jnp.ones((8, GROUP * TILE), BF)

    def forward(g, carry):
        left, right = [], []
        for j in range(GROUP):
            b = g * GROUP + j
            left.append(table[:, lanes(src[b])])
            block = adj[b]
            alive = b < live
            halves = []
            for t in range(2):
                keep = jnp.where(jnp.logical_and(alive, dst[b] == t), 1.0, 0.0)
                halves.append(block * jnp.full((TILE, TILE), keep, F32).astype(BF))
            right.append(jnp.concatenate(halves, axis=0))
        lhs = jnp.concatenate([jnp.concatenate(left, axis=1), ones], axis=0)
        gathered[...] += dot(lhs, jnp.concatenate(right, axis=1), 1, 1)
        return carry

    lax.fori_loop(0, groups, forward, 0)
    degree = gathered[F : F + 1, :]
    mean = (gathered[:F, :] / degree).astype(BF)
    start = pl.multiple_of(first[0], OWNED)
    own = table[:, pl.ds(start, OWNED)]
    pre = dot(own, w_self[...], 0, 0) + dot(mean, w_neigh[...], 0, 0) + bias[...]
    sig = jax.nn.sigmoid(pre)
    act[...] = (pre * sig).astype(BF)
    grad_pre = (grad_out[...].astype(F32) * sig * (1.0 + pre * (1.0 - sig))).astype(BF)
    part_bias = jnp.sum(grad_pre.astype(F32), axis=0, keepdims=True)

    row, col = iota((F, F), 0), iota((F, F), 1)
    x_of, y_of = (col // ROWS) % X, col // (ROWS * X)
    order = (row == x_of * (Y * ROWS) + y_of * ROWS + col % ROWS).astype(F32).astype(BF)

    def reorder(value):
        return dot(order, value, 1, 0).astype(BF)

    for k, value in enumerate((own, mean)):
        high, low = split(dot(value, grad_pre, 1, 0))
        at = COLS + k * H
        out[:, at : at + H] = reorder(high)
        out[:, at + WIDE : at + WIDE + H] = reorder(low)
    per = H // MEMBERS
    mine = iota((F, H), 1) // per == iota((F, H), 0) // ROWS
    squeeze = (iota((H, TILE), 0) % per == iota((H, TILE), 1)).astype(F32).astype(BF)
    for k, value in enumerate(split(part_bias)):
        spread = jnp.where(mine, value.astype(F32), 0.0).astype(BF)
        at = COLS + k * WIDE + 2 * H
        out[:, at : at + TILE] = reorder(dot(spread, squeeze, 1, 0).astype(BF))

    from_self = dot(reorder(w_self[...]), grad_pre, 1, 1)
    grad_mean = (dot(reorder(w_neigh[...]), grad_pre, 1, 1) / degree).astype(BF)
    pair = (grad_mean[:, :TILE], grad_mean[:, TILE:])
    terms[...] = jnp.zeros_like(terms)
    terms[:, pl.ds(start, OWNED)] = from_self

    def backward(g, carry):
        for j in range(GROUP):
            b = g * GROUP + j
            keep = jnp.where(b < live, 1.0, 0.0)
            second = jnp.full((F, TILE), dst[b], jnp.int32) == 1
            value = jnp.where(second, pair[1].astype(F32), pair[0].astype(F32)) * keep
            terms[:, lanes(src[b])] += dot(value.astype(BF), adj[b], 1, 0)
        return carry

    lax.fori_loop(0, groups, backward, 0)

    def narrow(n, carry):
        at = pl.ds(pl.multiple_of(n * 1024, 1024), 1024)
        out[:, at] = terms[:, at].astype(BF)
        return carry

    lax.fori_loop(0, COLS // 1024, narrow, 0)


def first_sum_kernel(parts, out):
    rows = F // X

    def total(at):
        return sum(parts[x * rows : (x + 1) * rows, at].astype(F32) for x in range(X))

    def put(value, at):
        for y in range(Y):
            out[y, :, at] = value[y * ROWS : (y + 1) * ROWS, :]

    def step(n, carry):
        at = pl.ds(pl.multiple_of(n * 512, 512), 512)
        put(total(at).astype(BF), at)
        return carry

    lax.fori_loop(0, COLS // 512, step, 0)
    high_at, low_at = pl.ds(COLS, WIDE), pl.ds(COLS + WIDE, WIDE)
    high, low = split(total(high_at) + total(low_at))
    put(high, high_at)
    put(low, low_at)


def second_sum_kernel(parts, own, away):
    def total(at, width):
        return sum(parts[y, :, at : at + width].astype(F32) for y in range(Y))

    for at in range(0, OWN * TILE, 1024):
        own[:, at : at + 1024] = total(at, 1024)
    for slab in range(SLABS):
        for slot in range(SLOTS):
            tile = total((OWN + slab * SLOTS + slot) * TILE, TILE)
            away[slab, slot * ROWS : (slot + 1) * ROWS, :] = tile.astype(BF)
    both = split(total(COLS, WIDE) + total(COLS + WIDE, WIDE))
    base = SLOTS * ROWS
    for value in both:
        for k in range(GRADS):
            piece = value[:, k * TILE : (k + 1) * TILE]
            for slab in range(SLABS):
                away[slab, base : base + ROWS, :] = piece
            base += ROWS


def land_kernel(send, own, back, out, grads):
    out[...] = own[...]
    for slab in range(SLABS):
        for slot in range(SLOTS):
            tile = back[slab, slot * ROWS : (slot + 1) * ROWS, :].astype(F32)
            out[:, lanes(send[slab * SLOTS + slot])] += tile
    base = SLOTS * ROWS
    for k in range(GRADS):
        at = base + k * ROWS
        low = at + GRADS * ROWS
        value = sum(
            back[slab, at : at + ROWS, :].astype(F32) + back[slab, low : low + ROWS, :].astype(F32)
            for slab in range(SLABS)
        )
        for m in range(MEMBERS):
            grads[m, :, k * TILE : (k + 1) * TILE] = value


def local(
    node_feats,
    w_self,
    w_neigh,
    out_bias,
    adjacency,
    block_dst,
    block_src,
    block_count,
    send_list,
    grad_out,
):
    send = send_list.reshape(-1)
    first = (lax.axis_index(("y", "x")) * OWNED).astype(jnp.int32).reshape(1)
    outgoing = call(pick_kernel, [SMEM, VMEM], struct((SLABS, SLOTS * ROWS, TILE), BF))(
        send, node_feats
    )
    incoming = lax.all_to_all(outgoing, ("z", "c"), 0, 0, tiled=True)
    table = call(table_kernel, [VMEM, VMEM], struct((ROWS, COLS), BF))(node_feats, incoming)
    table = lax.all_gather(table, "x", axis=0, tiled=True)
    table = lax.all_gather(table, "y", axis=0, tiled=True)
    activated, terms = call(
        layer_kernel,
        [SMEM] * 4 + [VMEM] * 6,
        (struct((OWNED, H), BF), struct((F, FULL), BF)),
        (pltpu.VMEM((F + 8, OWNED), F32), pltpu.VMEM((F, COLS), F32)),
    )(
        block_src,
        block_dst,
        block_count,
        first,
        table,
        adjacency,
        w_self,
        w_neigh,
        out_bias.reshape(1, H),
        grad_out,
    )
    terms = lax.all_to_all(terms, "x", 0, 0, tiled=True)
    terms = call(first_sum_kernel, [VMEM], struct((Y, ROWS, FULL), BF))(terms)
    terms = lax.all_to_all(terms, "y", 0, 0, tiled=True)
    own, away = call(
        second_sum_kernel,
        [VMEM],
        (
            struct((ROWS, OWN * TILE), F32),
            struct((SLABS, SLOTS * ROWS + 2 * GRADS * ROWS, TILE), BF),
        ),
    )(terms)
    back = lax.all_to_all(away, ("z", "c"), 0, 0, tiled=True)
    grad_feats, grads = call(
        land_kernel,
        [SMEM, VMEM, VMEM],
        (struct((ROWS, OWN * TILE), F32), struct((MEMBERS, ROWS, WIDE), F32)),
    )(send, own, back)
    grads = lax.all_to_all(grads, ("y", "x"), 0, 0, tiled=True)
    grad_self = grads[:, :, :H].reshape(F, H)
    grad_neigh = grads[:, :, H : 2 * H].reshape(F, H)
    grad_bias = grads[:, 0, 2 * H : 2 * H + H // MEMBERS].reshape(H)
    return activated, grad_feats, grad_self, grad_neigh, grad_bias


def solution(mesh):
    grid = Mesh(mesh.devices.reshape(Z, C, Y, X), ("z", "c", "y", "x"))
    vert, feat = ("z", "c"), ("y", "x")
    every = vert + feat
    in_specs = (
        P(feat, vert),
        P(),
        P(),
        P(),
        P(every, None, None),
        P(every),
        P(every),
        P(every),
        P(vert, None, None),
        P(every, None),
    )
    out_specs = (P(every, None), P(feat, vert), P(), P(), P())
    return jax.shard_map(local, mesh=grid, in_specs=in_specs, out_specs=out_specs, check_vma=False)
```

time: 880 us -> 256 us (0.29)
  waiting for transfers between devices: 651 us -> 50.5 us
  matrix products: 28.1 us -> 0 us
  blocking collectives: 136 us -> 163 us
  starting transfers between devices: 15.4 us -> 0.04 us
  local copies, waits for them, and re-layouts: 25.8 us -> 14 us
  Pallas kernels: 0 us -> 10.5 us
    psum x1 -> x0, waiting for transfers between devices: 350 us -> none  [local(): lax.psum((part_self, part_neigh, part_bias), ('vert', 'feat'))]
    reduce_scatter x1 -> x0, waiting for transfers between devices: 224 us -> none  [local(): lax.psum_scatter(lax.dynamic_update_slice_in_dim(dev_terms, placed, first...]
    all_to_all x1 -> x5, blocking collectives: 26.6 us -> 152 us  [the longest x1 48.6 us: local(): terms = lax.all_to_all(terms, 'x', 0, 0, tiled=True)]
    psum x1 -> x0, blocking collectives: 109 us -> none  [local(): lax.psum((part_self, part_neigh, part_bias), ('vert', 'feat'))]
    dot_general x14 -> x0, matrix products: 28.1 us -> none  [the longest x1 7.28 us: local(): jnp.einsum('bn,cbk->cnk', src_onehot, backward, precision=lax.Precision.H...]
    all_gather x1, waiting for transfers between devices: 77.2 us -> 50.5 us  [local(): table = lax.all_gather(table, 'y', axis=0, tiled=True)]
    all_to_all x1 -> x0, starting transfers between devices: 15.2 us -> none  [local(): lax.all_to_all(away.astype(jnp.bfloat16), 'vert', split_axis=1, concat_ax...]
    all_gather x0 -> x1, blocking collectives: none -> 11 us  [local(): table = lax.all_gather(table, 'x', axis=0, tiled=True)]
  transfers between devices with their start and end apart: 4 -> 1, of which waited for: 3 -> 1; matrix products, arithmetic and copies ran while one was open for 1% -> 0% of each run, Pallas kernels for 0% -> 0%
where the time goes in v1:
time: 256 us; the launch traced here: 253 us
  blocking collectives  163 us (64%)
  waiting for transfers between devices  50.5 us (20%)
  between operations  14.7 us (6%)
  local copies, waits for them, and re-layouts  14 us (5%)
  Pallas kernels  10.5 us (4%)
    all_gather x1, waiting for transfers between devices, local(): table = lax.all_gather(table, 'y', axis=0, tiled=True)  50.5 us
    all_to_all x1, blocking collectives, local(): terms = lax.all_to_all(terms, 'x', 0, 0, tiled=True)  48.6 us
    all_to_all x1, blocking collectives, local(): terms = lax.all_to_all(terms, 'y', 0, 0, tiled=True)  34.4 us
    all_to_all x1, blocking collectives, local(): back = lax.all_to_all(away, ('z', 'c'), 0, 0, tiled=True)  28.5 us
    all_to_all x1, blocking collectives, local(): incoming = lax.all_to_all(outgoing, ('z', 'c'), 0, 0, tiled=True)  26.6 us
    all_to_all x1, blocking collectives, local(): grads = lax.all_to_all(grads, ('y', 'x'), 0, 0, tiled=True)  14.1 us
    unnamed x22, local copies, waits for them, and re-layouts  11.8 us
    all_gather x1, blocking collectives, local(): table = lax.all_gather(table, 'x', axis=0, tiled=True)  11 us
  transfers between devices with their start and end apart: 1, of which 1 were waited for; matrix products, arithmetic and copies ran while one was open for 0% of the time, Pallas kernels for 0%

profile of v1, /device:TPU:1, one launch (start us, length us, event | category | flops | bytes accessed | tf_op | source)
XLA Modules:
  0.0 253.1 jit_solution(5111662673466575301)
XLA Ops:
  7.2 0.0 all-gather.3.cloned.1.call-start
  7.2 0.8 copy.17
  8.0 0.1 reshape.28.send
  8.1 0.0 copy-start.2
  8.1 0.8 copy-done.2
  8.9 0.6 shard_map.137
  9.5 26.6 %all_to_all.31.incoming = bf16[24,8,128]{2,1,0:T(8,128)(2,1)S(1)} all-to-all(bf16[24,8,128]{2,1,0:T(8,128)(2,1)S(1)} %shard_map.137), channel_id=1, replica_groups=mesh['z'=12,'c'=2,'y'=8,'x'=4] {'z','c'}, dimensions={0} | all-to-all | bytes 98304 | tf_op jit(solution)/shard_map/all_to_all | solution.py:241
  36.1 0.0 copy-start.3
  36.1 0.8 copy-done.3
  37.0 11.0 %all-gather = bf16[4,4,14336]{2,1,0:T(4,128)(2,1)S(1)} all-gather(bf16[1,4,14336]{2,1,0:T(4,128)(2,1)S(1)} %bitcast.7), channel_id=1, replica_groups=mesh['z'=12,'c'=2,'y'=8,'x'=4] {'x'}, dimensions={0}, use_global_device_ids=true | all-gather | bytes 573440 | tf_op jit(solution)/shard_map/all_gather | solution.py:243
  48.0 0.9 reshape.33
  48.8 0.0 all-gather.3.cloned.1.call-update
  49.5 50.5 %all-gather.3.cloned.1.call-done.table = bf16[128,14336]{1,0:T(8,128)(2,1)} async-done(((bf16[16,14336]{1,0:T(8,128)(2,1)}), bf16[128,14336]{1,0:T(8,128)(2,1)}) %all-gather.3.cloned.1.call-update) | async-done | bytes 3670032 | tf_op jit(solution)/shard_map/all_gather | solution.py:244
  100.0 2.0 copy-done
  102.1 1.9 copy-done.1
  104.0 0.9 copy-done.4
  104.9 0.8 copy-done.5
  105.7 0.8 copy-done.6
  106.6 0.7 copy-done.7
  107.2 0.7 copy-done.8
  107.9 0.7 copy-done.9
  108.5 7.5 %shard_map.139 = (bf16[256,256]{1,0:T(8,128)(2,1)}, bf16[128,15616]{1,0:T(8,128)(2,1)S(1)}) custom-call(s32[96]{0:T(128)S(1)} %copy-done.8, s32[96]{0:T(128)S(1)} %copy-done.9, s32[1]{0:T(128)S(6)} %copy.18.count, s32[1]{0:T(128)} %bitcast.first, bf16[128,14336]{1,0:T(8,128)(2,1)S(1)} %copy-done, bf16[96,128,128]{2,1,0:T(8,128)(2,1)S(1)} %copy-done.1, ...), custom_call_target="tpu_custom_call" | custom-call | tf_op jit(solution)/shard_map/pallas_call | solution.py:245
  116.0 48.6 %all_to_all.32 = bf16[4,32,15616]{2,1,0:T(8,128)(2,1)S(1)} all-to-all(bf16[4,32,15616]{2,1,0:T(8,128)(2,1)S(1)} %bitcast.6), channel_id=1, replica_groups=mesh['z'=12,'c'=2,'y'=8,'x'=4] {'x'}, dimensions={0} | all-to-all | bytes 7995392 | tf_op jit(solution)/shard_map/all_to_all | solution.py:262
  164.7 0.7 shard_map.140
  165.4 34.4 %all_to_all.33.parts = bf16[8,4,15616]{2,1,0:T(4,128)(2,1)S(1)} all-to-all(bf16[8,4,15616]{2,1,0:T(4,128)(2,1)S(1)} %shard_map.140), channel_id=1, replica_groups=mesh['z'=12,'c'=2,'y'=8,'x'=4] {'y'}, dimensions={0} | all-to-all | bytes 1998848 | tf_op jit(solution)/shard_map/all_to_all | solution.py:264
  199.8 0.2 shard_map.141
  200.0 28.5 %all_to_all.34.back = bf16[24,48,128]{2,1,0:T(8,128)(2,1)S(1)} all-to-all(bf16[24,48,128]{2,1,0:T(8,128)(2,1)S(1)} %get-tuple-element.14), channel_id=1, replica_groups=mesh['z'=12,'c'=2,'y'=8,'x'=4] {'z','c'}, dimensions={0} | all-to-all | bytes 589824 | tf_op jit(solution)/shard_map/all_to_all | solution.py:273
  228.6 1.4 shard_map.142
  230.0 14.1 %all_to_all.35 = f32[32,4,640]{2,1,0:T(4,128)S(1)} all-to-all(f32[32,4,640]{2,1,0:T(4,128)S(1)} %get-tuple-element.16), channel_id=1, replica_groups=mesh['z'=12,'c'=2,'y'=8,'x'=4] {'y','x'}, dimensions={0} | all-to-all | bytes 655360 | tf_op jit(solution)/shard_map/all_to_all | solution.py:279
  244.1 0.7 reshape_squeeze.3
  244.8 0.7 reshape.31
  245.5 0.7 reshape.30
  (11 shorter events, 0.1 us)
Async XLA Ops:
  7.2 92.9 %all-gather.3.cloned.1.call-start = ((), (), s32[]{:S(2)}) async-start(), calls=%async_computation.5 | async-start | bytes 4128768 | tf_op jit(solution)/shard_map/all_gather | solution.py:244
  8.1 0.8 copy-start.2
  36.1 0.8 copy-start.3
  100.0 2.0 copy-start
  102.1 1.9 copy-start.1
  104.0 0.9 copy-start.4
  104.9 0.8 copy-start.5
  105.7 0.8 copy-start.6
  106.6 0.7 copy-start.7
  107.2 0.7 copy-start.8
  107.9 0.7 copy-start.9
Sparse Core Ops, SparseCore 0:
  49.0 51.0 all-gather.2

commit v2 on v1

v2 whole, which is shorter than its diff:
```python
import functools

import jax
import jax.numpy as jnp
from jax import lax
from jax.experimental import pallas as pl
from jax.experimental.pallas import tpu as pltpu
from jax.sharding import Mesh
from jax.sharding import PartitionSpec as P

X, Y, Z, C = 4, 8, 12, 2
MEMBERS = X * Y
SLABS = Z * C
F = 128
H = 256
TILE = 128
SLOTS = 2
OWN = 64
AWAY = SLABS * SLOTS
TABLE = OWN + AWAY
ROWS = F // MEMBERS
BPD = 96
OWNED = 2 * TILE
COLS = TABLE * TILE
OWN_COLS = OWN * TILE
AWAY_COLS = AWAY * TILE
CHUNK = 24
GRAD_ROWS = SLABS * CHUNK
GROUP = 8
FETCHES = 4
FETCH = BPD // FETCHES

BF = jnp.bfloat16
F32 = jnp.float32
VMEM = pl.BlockSpec(memory_space=pltpu.VMEM)
SMEM = pl.BlockSpec(memory_space=pltpu.SMEM)
HBM = pl.BlockSpec(memory_space=pltpu.HBM)
LIMIT = 40 * 1024 * 1024
FULL_LIMIT = 62 * 1024 * 1024


def call(body, ins, outs, scratch=(), places=None, limit=LIMIT):
    return pl.pallas_call(
        body,
        in_specs=ins,
        out_specs=jax.tree.map(lambda _: VMEM, outs) if places is None else places,
        out_shape=outs,
        scratch_shapes=scratch,
        compiler_params=pltpu.CompilerParams(vmem_limit_bytes=limit),
    )


def struct(shape, dtype):
    return jax.ShapeDtypeStruct(shape, dtype)


def lanes(at):
    return pl.ds(pl.multiple_of(at * TILE, TILE), TILE)


def pick_kernel(send, feats, out):
    for slab in range(SLABS):
        for slot in range(SLOTS):
            tile = feats[:, lanes(send[slot, slab])]
            out[slab, slot * ROWS : (slot + 1) * ROWS, :] = tile


def table_kernel(feats, incoming, out):
    out[:, :OWN_COLS] = feats[...]
    for slab in range(SLABS):
        for slot in range(SLOTS):
            at = OWN_COLS + (slab * SLOTS + slot) * TILE
            out[:, at : at + TILE] = incoming[slab, slot * ROWS : (slot + 1) * ROWS, :]


def dot(a, b, ca, cb):
    return lax.dot_general(a, b, (((ca,), (cb,)), ((), ())), preferred_element_type=F32)


def iota(shape, axis):
    return lax.broadcasted_iota(jnp.int32, shape, axis)


def layer_kernel(
    src,
    dst,
    count,
    first,
    table_hbm,
    adj_hbm,
    w_self_hbm,
    w_neigh_hbm,
    bias_hbm,
    grad_out_hbm,
    act,
    out_hbm,
    grads,
    out,
    table,
    adj,
    w_self,
    w_neigh,
    bias,
    grad_out,
    gathered,
    terms,
    sems,
):
    def fetch(k, source, target):
        copy = pltpu.make_async_copy(source, target, sems.at[k])
        copy.start()
        return copy

    get_table = fetch(0, table_hbm, table)
    get_adj = [
        fetch(1 + k, adj_hbm.at[pl.ds(k * FETCH, FETCH)], adj.at[pl.ds(k * FETCH, FETCH)])
        for k in range(FETCHES)
    ]
    rest = [
        fetch(1 + FETCHES + k, source, target)
        for k, (source, target) in enumerate(
            (
                (w_self_hbm, w_self),
                (w_neigh_hbm, w_neigh),
                (bias_hbm, bias),
                (grad_out_hbm, grad_out),
            )
        )
    ]

    row, col = iota((F, F), 0), iota((F, F), 1)

    x_of, y_of = (col // ROWS) % X, col // (ROWS * X)
    order = (row == x_of * (Y * ROWS) + y_of * ROWS + col % ROWS).astype(F32).astype(BF)
    live = count[0]
    gathered[...] = jnp.zeros_like(gathered)
    ones = jnp.ones((8, GROUP * TILE), BF)
    get_table.wait()

    def forward(g, carry):
        left, right = [], []
        for j in range(GROUP):
            b = g * GROUP + j
            left.append(table[:, lanes(src[b])])
            block = adj[b]
            alive = b < live
            halves = []
            for t in range(2):
                keep = jnp.where(jnp.logical_and(alive, dst[b] == t), 1.0, 0.0)
                halves.append(block * jnp.full((TILE, TILE), keep, F32).astype(BF))
            right.append(jnp.concatenate(halves, axis=0))
        lhs = jnp.concatenate([jnp.concatenate(left, axis=1), ones], axis=0)
        gathered[...] += dot(lhs, jnp.concatenate(right, axis=1), 1, 1)
        return carry

    groups = lax.div(live + (GROUP - 1), GROUP)
    per = FETCH // GROUP
    for k in range(FETCHES):
        get_adj[k].wait()
        lax.fori_loop(k * per, jnp.minimum(groups, (k + 1) * per), forward, 0)
    for copy in rest:
        copy.wait()
    degree = gathered[F : F + 1, :]
    mean = (gathered[:F, :] / degree).astype(BF)
    start = pl.multiple_of(first[0], OWNED)
    own = table[:, pl.ds(start, OWNED)]
    pre = dot(own, w_self[...], 0, 0) + dot(mean, w_neigh[...], 0, 0) + bias[...]
    sig = jax.nn.sigmoid(pre)
    act[...] = (pre * sig).astype(BF)
    grad_pre = (grad_out[...].astype(F32) * sig * (1.0 + pre * (1.0 - sig))).astype(BF)

    at = 0
    for value in (own, mean):
        part = dot(value, grad_pre, 1, 0)
        for k in range(H // TILE):
            grads[at : at + F, :] = part[:, k * TILE : (k + 1) * TILE]
            at += F
    part_bias = jnp.sum(grad_pre.astype(F32), axis=0, keepdims=True)
    grads[at:, :] = jnp.zeros((GRAD_ROWS - at, TILE), F32)
    for k in range(H // TILE):
        grads[at + k : at + k + 1, :] = part_bias[:, k * TILE : (k + 1) * TILE]

    def reorder(value):
        return dot(order, value, 1, 0).astype(BF)

    from_self = dot(reorder(w_self[...]), grad_pre, 1, 1)
    grad_mean = (dot(reorder(w_neigh[...]), grad_pre, 1, 1) / degree).astype(BF)
    pair = (grad_mean[:, :TILE], grad_mean[:, TILE:])
    terms[...] = jnp.zeros_like(terms)
    terms[:, pl.ds(start, OWNED)] = from_self

    def backward(g, carry):
        for j in range(GROUP):
            b = g * GROUP + j
            keep = jnp.where(b < live, 1.0, 0.0)
            second = jnp.full((F, TILE), dst[b], jnp.int32) == 1
            value = jnp.where(second, pair[1].astype(F32), pair[0].astype(F32)) * keep
            terms[:, lanes(src[b])] += dot(value.astype(BF), adj[b], 1, 0)
        return carry

    lax.fori_loop(0, groups, backward, 0)

    def narrow(n, carry):
        at = pl.ds(pl.multiple_of(n * 1024, 1024), 1024)
        out[:, at] = terms[:, at].astype(BF)
        return carry

    lax.fori_loop(0, COLS // 1024, narrow, 0)
    put = pltpu.make_async_copy(out, out_hbm, sems.at[0])
    put.start()
    put.wait()


def cut_kernel(terms, out):
    for y in range(Y):
        out[y] = terms[y * ROWS : (y + 1) * ROWS, :]


def spread_kernel(parts, out):
    total = sum(parts[k] for k in range(SLABS))
    for m in range(MEMBERS):
        out[m] = total


def sum_kernel(parts, grads, own, away):
    def total(at, width):
        return sum(parts[y, :, at : at + width].astype(F32) for y in range(Y))

    for at in range(0, OWN_COLS, 1024):
        own[:, at : at + 1024] = total(at, 1024)
    whole = sum(grads[m] for m in range(MEMBERS)).astype(BF)
    for slab in range(SLABS):
        for slot in range(SLOTS):
            tile = total(OWN_COLS + (slab * SLOTS + slot) * TILE, TILE)
            away[slab, slot * ROWS : (slot + 1) * ROWS, :] = tile.astype(BF)
        away[slab, SLOTS * ROWS :, :] = whole


def land_kernel(send, own, back, out, grad_self, grad_neigh, grad_bias):
    out[...] = own[...]
    for slab in range(SLABS):
        for slot in range(SLOTS):
            tile = back[slab, slot * ROWS : (slot + 1) * ROWS, :].astype(F32)
            out[:, lanes(send[slot, slab])] += tile
    for slab in range(SLABS):
        value = back[slab, SLOTS * ROWS :, :].astype(F32)
        for k in range(0, CHUNK, 8):
            block, at = divmod(slab * CHUNK + k, F)
            if block < 4:
                target = (grad_self, grad_neigh)[block // 2]
                lane = (block % 2) * TILE
                target[at : at + 8, lane : lane + TILE] = value[k : k + 8]
            elif at == 0:
                for half in range(2):
                    grad_bias[:, half * TILE : (half + 1) * TILE] = value[k + half : k + half + 1]


def local(
    node_feats,
    w_self,
    w_neigh,
    out_bias,
    adjacency,
    block_dst,
    block_src,
    block_count,
    send_list,
    grad_out,
):
    vert, feat = ("z", "c"), ("y", "x")
    send = jnp.swapaxes(send_list[0], 0, 1)
    first = (lax.axis_index(feat) * OWNED).astype(jnp.int32).reshape(1)
    outgoing = call(pick_kernel, [SMEM, VMEM], struct((SLABS, SLOTS * ROWS, TILE), BF))(
        send, node_feats
    )
    incoming = lax.all_to_all(outgoing, vert, 0, 0, tiled=True)
    table = call(table_kernel, [VMEM, VMEM], struct((ROWS, COLS), BF))(node_feats, incoming)
    table = lax.all_gather(table, "x", axis=0, tiled=True)
    table = lax.all_gather(table, "y", axis=0, tiled=True)
    activated, terms, grads = call(
        layer_kernel,
        [SMEM] * 4 + [HBM] * 6,
        (struct((OWNED, H), BF), struct((F, COLS), BF), struct((GRAD_ROWS, TILE), F32)),
        (
            pltpu.VMEM((F, COLS), BF),
            pltpu.VMEM((F, COLS), BF),
            pltpu.VMEM((BPD, TILE, TILE), BF),
            pltpu.VMEM((F, H), BF),
            pltpu.VMEM((F, H), BF),
            pltpu.VMEM((1, H), F32),
            pltpu.VMEM((OWNED, H), BF),
            pltpu.VMEM((F + 8, OWNED), F32),
            pltpu.VMEM((F, COLS), F32),
            pltpu.SemaphoreType.DMA((1 + FETCHES + 4,)),
        ),
        (VMEM, HBM, VMEM),
        FULL_LIMIT,
    )(
        block_src,
        block_dst,
        block_count,
        first,
        table,
        adjacency,
        w_self,
        w_neigh,
        out_bias.reshape(1, H),
        grad_out,
    )
    terms = lax.psum_scatter(terms, "x", scatter_dimension=0, tiled=True)
    grads = grads.reshape(SLABS, CHUNK, TILE)
    grads = lax.all_to_all(grads, vert, 0, 0, tiled=True)
    grads = call(spread_kernel, [VMEM], struct((MEMBERS, CHUNK, TILE), F32))(grads)
    grads = lax.all_to_all(grads, feat, 0, 0, tiled=True)
    terms, grads = lax.optimization_barrier((terms, grads))
    terms = call(cut_kernel, [VMEM], struct((Y, ROWS, COLS), BF))(terms)
    terms = lax.all_to_all(terms, "y", 0, 0, tiled=True)
    own, away = call(
        sum_kernel,
        [VMEM, VMEM],
        (struct((ROWS, OWN_COLS), F32), struct((SLABS, SLOTS * ROWS + CHUNK, TILE), BF)),
    )(terms, grads)
    back = lax.all_to_all(away, vert, 0, 0, tiled=True)
    grad_feats, grad_self, grad_neigh, grad_bias = call(
        land_kernel,
        [SMEM, VMEM, VMEM],
        (
            struct((ROWS, OWN_COLS), F32),
            struct((F, H), F32),
            struct((F, H), F32),
            struct((1, H), F32),
        ),
    )(send, own, back)
    return activated, grad_feats, grad_self, grad_neigh, grad_bias.reshape(H)


def solution(mesh):
    grid = Mesh(mesh.devices.reshape(Z, C, Y, X), ("z", "c", "y", "x"))
    vert, feat = ("z", "c"), ("y", "x")
    every = vert + feat
    in_specs = (
        P(feat, vert),
        P(),
        P(),
        P(),
        P(every, None, None),
        P(every),
        P(every),
        P(every),
        P(vert, None, None),
        P(every, None),
    )
    out_specs = (P(every, None), P(feat, vert), P(), P(), P())
    return jax.shard_map(local, mesh=grid, in_specs=in_specs, out_specs=out_specs, check_vma=False)
```

time: 256 us -> 235 us (0.918); the launches traced: 253 us -> 235 us
  blocking collectives: 163 us -> 140 us
  local copies, waits for them, and re-layouts: 14 us -> 5.34 us
  waiting for transfers between devices: 50.5 us -> 58.4 us
  Pallas kernels: 10.5 us -> 16.3 us
    all_to_all x4, blocking collectives: 118 us -> 98 us  [the longest x1 26.7 us: local(): grads = lax.all_to_all(grads, vert, 0, 0, tiled=True)]
    reduce_scatter x0 -> x1, waiting for transfers between devices: none -> 7.85 us  [local(): terms = lax.psum_scatter(terms, 'x', scatter_dimension=0, tiled=True)]
    unnamed x22 -> x13, local copies, waits for them, and re-layouts: 11.8 us -> 5.34 us
    pallas_call x4 -> x5, Pallas kernels: 9.87 us -> 15.6 us  [the longest x1 13.7 us: local(): call(layer_kernel, [SMEM] * 4 + [HBM] * 6, (struct((OWNED, H), BF), struc...]
    all_to_all x1, blocking collectives: 34.4 us -> 31.1 us  [local(): terms = lax.all_to_all(terms, 'y', 0, 0, tiled=True)]
  transfers between devices with their start and end apart: 1 -> 2, of which waited for: 1 -> 2; matrix products, arithmetic and copies ran while one was open for 0% -> 0% of each run, Pallas kernels for 0% -> 0%
where the time goes in v2:
time: 235 us
  blocking collectives  140 us (60%)
  waiting for transfers between devices  58.4 us (25%)
  Pallas kernels  16.3 us (7%)
  between operations  14.7 us (6%)
  local copies, waits for them, and re-layouts  5.34 us (2%)
    all_gather x1, waiting for transfers between devices, local(): table = lax.all_gather(table, 'y', axis=0, tiled=True)  50.5 us
    all_to_all x1, blocking collectives, local(): terms = lax.all_to_all(terms, 'y', 0, 0, tiled=True)  31.1 us
    all_to_all x1, blocking collectives, local(): grads = lax.all_to_all(grads, vert, 0, 0, tiled=True)  26.7 us
    all_to_all x1, blocking collectives, local(): incoming = lax.all_to_all(outgoing, vert, 0, 0, tiled=True)  26.6 us
    all_to_all x1, blocking collectives, local(): back = lax.all_to_all(away, vert, 0, 0, tiled=True)  25.8 us
    all_to_all x1, blocking collectives, local(): grads = lax.all_to_all(grads, feat, 0, 0, tiled=True)  19 us
    pallas_call x1, Pallas kernels, local(): call(layer_kernel, [SMEM] * 4 + [HBM] * 6, (struct((OWNED, H), BF), struc...  13.7 us
    all_gather x1, blocking collectives, local(): table = lax.all_gather(table, 'x', axis=0, tiled=True)  11 us
  transfers between devices with their start and end apart: 2, of which 2 were waited for; matrix products, arithmetic and copies ran while one was open for 0% of the time, Pallas kernels for 0%

profile of v2, /device:TPU:1, one launch (start us, length us, event | category | flops | bytes accessed | tf_op | source)
XLA Modules:
  0.0 234.9 jit_solution(15360463462366989489)
XLA Ops:
  7.2 0.0 all-gather.3.cloned.1.call-start
  7.2 0.0 copy-start.1
  7.2 0.8 copy-done.1
  8.1 0.0 copy-start.3
  8.1 0.7 copy-done.3
  8.7 0.6 shard_map.137
  9.4 26.6 %all_to_all.25.incoming = bf16[24,8,128]{2,1,0:T(8,128)(2,1)S(1)} all-to-all(bf16[24,8,128]{2,1,0:T(8,128)(2,1)S(1)} %shard_map.137), channel_id=1, replica_groups=mesh['z'=12,'c'=2,'y'=8,'x'=4] {'z','c'}, dimensions={0} | all-to-all | bytes 98304 | tf_op jit(solution)/shard_map/all_to_all | solution.py:276
  35.9 0.0 copy-start.2
  35.9 0.8 copy-done.2
  36.8 11.0 %all-gather = bf16[4,4,14336]{2,1,0:T(4,128)(2,1)S(1)} all-gather(bf16[1,4,14336]{2,1,0:T(4,128)(2,1)S(1)} %bitcast.8), channel_id=1, replica_groups=mesh['z'=12,'c'=2,'y'=8,'x'=4] {'x'}, dimensions={0}, use_global_device_ids=true | all-gather | bytes 573440 | tf_op jit(solution)/shard_map/all_gather | solution.py:278
  47.8 0.9 reshape.27
  48.7 0.0 all-gather.3.cloned.1.call-update
  48.7 0.0 reduce-scatter.2.cloned.1.call-start
  49.4 50.5 %all-gather.3.cloned.1.call-done.table_hbm = bf16[128,14336]{1,0:T(8,128)(2,1)} async-done(((bf16[16,14336]{1,0:T(8,128)(2,1)}), bf16[128,14336]{1,0:T(8,128)(2,1)}) %all-gather.3.cloned.1.call-update) | async-done | bytes 3670032 | tf_op jit(solution)/shard_map/all_gather | solution.py:279
  99.9 13.7 %shard_map.139 = (bf16[256,256]{1,0:T(8,128)(2,1)}, bf16[128,14336]{1,0:T(8,128)(2,1)}, f32[576,128]{1,0:T(8,128)}) custom-call(s32[96]{0:T(128)} %src.1, s32[96]{0:T(128)} %dst.1, s32[1]{0:T(128)S(6)} %copy.15.count, s32[1]{0:T(128)} %bitcast.first, bf16[128,14336]{1,0:T(8,128)(2,1)} %all-gather.3.cloned.1.call-done.table_hbm, ...), custom_call_target="tpu_custom_call" | custom-call | tf_op jit(solution)/shard_map/pallas_call | solution.py:280
  113.6 0.0 copy-start.5
  113.6 0.0 reduce-scatter.2.cloned.1.call-update
  113.7 0.9 copy-done.5
  114.6 0.0 copy-start.4
  114.6 26.7 %all_to_all.26.parts = f32[24,24,128]{2,1,0:T(8,128)S(1)} all-to-all(f32[24,24,128]{2,1,0:T(8,128)S(1)} %bitcast.11), channel_id=1, replica_groups=mesh['z'=12,'c'=2,'y'=8,'x'=4] {'z','c'}, dimensions={0} | all-to-all | bytes 589824 | tf_op jit(solution)/shard_map/all_to_all | solution.py:312
  141.3 0.1 shard_map.140
  141.3 19.0 %all_to_all.27.grads = f32[32,24,128]{2,1,0:T(8,128)S(1)} all-to-all(f32[32,24,128]{2,1,0:T(8,128)S(1)} %shard_map.140), channel_id=1, replica_groups=mesh['z'=12,'c'=2,'y'=8,'x'=4] {'y','x'}, dimensions={0} | all-to-all | bytes 786432 | tf_op jit(solution)/shard_map/all_to_all | solution.py:314
  160.3 7.9 %reduce-scatter.2.cloned.1.call-done.terms = bf16[32,14336]{1,0:T(8,128)(2,1)} async-done(((bf16[128,14336]{1,0:T(8,128)(2,1)}), bf16[32,14336]{1,0:T(8,128)(2,1)}) %reduce-scatter.2.cloned.1.call-update) | async-done | bytes 917520 | tf_op jit(solution)/shard_map/reduce_scatter | solution.py:310
  168.2 0.0 copy-start
  168.2 1.2 copy-done
  169.4 0.2 shard_map.141
  169.6 31.1 %all_to_all.28.parts = bf16[8,4,14336]{2,1,0:T(4,128)(2,1)S(1)} all-to-all(bf16[8,4,14336]{2,1,0:T(4,128)(2,1)S(1)} %shard_map.141), channel_id=1, replica_groups=mesh['z'=12,'c'=2,'y'=8,'x'=4] {'y'}, dimensions={0} | all-to-all | bytes 1835008 | tf_op jit(solution)/shard_map/all_to_all | solution.py:317
  200.7 0.2 shard_map.142
  200.9 25.8 %all_to_all.29.back = bf16[24,32,128]{2,1,0:T(8,128)(2,1)S(1)} all-to-all(bf16[24,32,128]{2,1,0:T(8,128)(2,1)S(1)} %get-tuple-element.22), channel_id=1, replica_groups=mesh['z'=12,'c'=2,'y'=8,'x'=4] {'z','c'}, dimensions={0} | all-to-all | bytes 393216 | tf_op jit(solution)/shard_map/all_to_all | solution.py:323
  226.7 0.0 copy-done.4
  226.7 1.4 shard_map.143
  (1 shorter events, 0.0 us)
Async XLA Ops:
  7.2 92.7 %all-gather.3.cloned.1.call-start = ((), (), s32[]{:S(2)}) async-start(), calls=%async_computation.6 | async-start | bytes 4128768 | tf_op jit(solution)/shard_map/all_gather | solution.py:279
  7.2 0.8 copy-start.1
  8.1 0.7 copy-start.3
  35.9 0.8 copy-start.2
  48.7 119.5 %reduce-scatter.2.cloned.1.call-start = ((), (), s32[]{:S(2)}) async-start(), calls=%async_computation.7 | async-start | bytes 4587520 | tf_op jit(solution)/shard_map/reduce_scatter | solution.py:310
  113.6 1.0 copy-start.5
  114.6 112.1 %copy-start.4 = (s32[1,24,2]{1,2,0:T(2,128)S(1)}, s32[1,24,2]{1,2,0:T(2,128)}, u32[]{:S(2)}) copy-start(s32[1,24,2]{1,2,0:T(2,128)} %param.18) | copy-start | bytes 580
  168.2 1.2 copy-start
Sparse Core Ops, SparseCore 0:
  48.8 51.0 all-gather.2
  113.8 54.3 reduce-scatter.1

commit v3 on v2

--- a/solution.py
+++ b/solution.py
@@ -24,11 +24,13 @@
 COLS = TABLE * TILE
 OWN_COLS = OWN * TILE
 AWAY_COLS = AWAY * TILE
-CHUNK = 24
-GRAD_ROWS = SLABS * CHUNK
+WIDE = 2 * H + TILE
+PER = H // MEMBERS
+EXTRA = X * 2 * H + TILE
 GROUP = 8
 FETCHES = 4
 FETCH = BPD // FETCHES
+PIECE = COLS // 7
 
 BF = jnp.bfloat16
 F32 = jnp.float32
@@ -58,7 +60,8 @@
     return pl.ds(pl.multiple_of(at * TILE, TILE), TILE)
 
 
-def pick_kernel(send, feats, out):
+def pick_kernel(send, feats, out, same):
+    same[...] = feats[...]
     for slab in range(SLABS):
         for slot in range(SLOTS):
             tile = feats[:, lanes(send[slot, slab])]
@@ -104,6 +107,7 @@
     grad_out,
     gathered,
     terms,
+    means,
     sems,
 ):
     def fetch(k, source, target):
@@ -134,6 +138,7 @@
     order = (row == x_of * (Y * ROWS) + y_of * ROWS + col % ROWS).astype(F32).astype(BF)
     live = count[0]
     gathered[...] = jnp.zeros_like(gathered)
+    terms[...] = jnp.zeros_like(terms)
     ones = jnp.ones((8, GROUP * TILE), BF)
     get_table.wait()
 
@@ -169,90 +174,110 @@
     act[...] = (pre * sig).astype(BF)
     grad_pre = (grad_out[...].astype(F32) * sig * (1.0 + pre * (1.0 - sig))).astype(BF)
 
-    at = 0
-    for value in (own, mean):
+    for k, value in enumerate((own, mean)):
         part = dot(value, grad_pre, 1, 0)
-        for k in range(H // TILE):
-            grads[at : at + F, :] = part[:, k * TILE : (k + 1) * TILE]
-            at += F
+        for m in range(MEMBERS):
+            grads[m, :, k * H : (k + 1) * H] = part[m * ROWS : (m + 1) * ROWS, :]
     part_bias = jnp.sum(grad_pre.astype(F32), axis=0, keepdims=True)
-    grads[at:, :] = jnp.zeros((GRAD_ROWS - at, TILE), F32)
-    for k in range(H // TILE):
-        grads[at + k : at + k + 1, :] = part_bias[:, k * TILE : (k + 1) * TILE]
+    mine = iota((F, H), 1) // PER == iota((F, H), 0) // ROWS
+    squeeze = (iota((H, TILE), 0) % PER == iota((H, TILE), 1)).astype(F32).astype(BF)
+    spread, rest_of = jnp.zeros((F, TILE), F32), part_bias
+    for _ in range(3):
+        high = rest_of.astype(BF).astype(F32)
+        rest_of = rest_of - high
+        spread += dot(jnp.where(mine, high, 0.0).astype(BF), squeeze, 1, 0)
+    for m in range(MEMBERS):
+        grads[m, :, 2 * H :] = spread[m * ROWS : (m + 1) * ROWS, :]
 
     def reorder(value):
         return dot(order, value, 1, 0).astype(BF)
 
     from_self = dot(reorder(w_self[...]), grad_pre, 1, 1)
     grad_mean = (dot(reorder(w_neigh[...]), grad_pre, 1, 1) / degree).astype(BF)
-    pair = (grad_mean[:, :TILE], grad_mean[:, TILE:])
-    terms[...] = jnp.zeros_like(terms)
+    means[0] = grad_mean[:, :TILE]
+    means[1] = grad_mean[:, TILE:]
+    means[2] = jnp.zeros((F, TILE), BF)
     terms[:, pl.ds(start, OWNED)] = from_self
 
     def backward(g, carry):
         for j in range(GROUP):
             b = g * GROUP + j
-            keep = jnp.where(b < live, 1.0, 0.0)
-            second = jnp.full((F, TILE), dst[b], jnp.int32) == 1
-            value = jnp.where(second, pair[1].astype(F32), pair[0].astype(F32)) * keep
-            terms[:, lanes(src[b])] += dot(value.astype(BF), adj[b], 1, 0)
+            value = means[jnp.where(b < live, dst[b], 2)]
+            terms[:, lanes(src[b])] += dot(value, adj[b], 1, 0)
         return carry
 
     lax.fori_loop(0, groups, backward, 0)
 
-    def narrow(n, carry):
-        at = pl.ds(pl.multiple_of(n * 1024, 1024), 1024)
+    puts = []
+    for n in range(0, COLS, PIECE):
+        at = slice(n, n + PIECE)
         out[:, at] = terms[:, at].astype(BF)
-        return carry
-
-    lax.fori_loop(0, COLS // 1024, narrow, 0)
-    put = pltpu.make_async_copy(out, out_hbm, sems.at[0])
-    put.start()
-    put.wait()
-
-
-def cut_kernel(terms, out):
+        put = pltpu.make_async_copy(out.at[:, at], out_hbm.at[:, at], sems.at[n // PIECE])
+        put.start()
+        puts.append(put)
+    for put in puts:
+        put.wait()
+
+
+def feat_sum_kernel(parts, out):
+    total = sum(parts[m] for m in range(MEMBERS))
+    for k in range(SLABS):
+        out[k] = total
+
+
+def vert_sum_kernel(parts, out):
+    out[...] = sum(parts[k] for k in range(SLABS))
+
+
+def join_kernel(terms, grads, out):
     for y in range(Y):
-        out[y] = terms[y * ROWS : (y + 1) * ROWS, :]
-
-
-def spread_kernel(parts, out):
-    total = sum(parts[k] for k in range(SLABS))
-    for m in range(MEMBERS):
-        out[m] = total
-
-
-def sum_kernel(parts, grads, own, away):
+        out[y, :, :COLS] = terms[y * ROWS : (y + 1) * ROWS, :]
+    bias = grads[0, :, 2 * H :]
+    for x in range(1, X):
+        bias += pltpu.roll(grads[x, :, 2 * H :], x * PER, 1)
+    bias = bias.astype(BF)
+    for x in range(X):
+        value = grads[x, :, : 2 * H].astype(BF)
+        at = COLS + x * 2 * H
+        for y in range(Y):
+            out[y, :, at : at + 2 * H] = value
+    for y in range(Y):
+        out[y, :, COLS + X * 2 * H :] = bias
+
+
+def sum_kernel(parts, own, away, extra):
     def total(at, width):
         return sum(parts[y, :, at : at + width].astype(F32) for y in range(Y))
 
     for at in range(0, OWN_COLS, 1024):
         own[:, at : at + 1024] = total(at, 1024)
-    whole = sum(grads[m] for m in range(MEMBERS)).astype(BF)
     for slab in range(SLABS):
         for slot in range(SLOTS):
             tile = total(OWN_COLS + (slab * SLOTS + slot) * TILE, TILE)
             away[slab, slot * ROWS : (slot + 1) * ROWS, :] = tile.astype(BF)
-        away[slab, SLOTS * ROWS :, :] = whole
-
-
-def land_kernel(send, own, back, out, grad_self, grad_neigh, grad_bias):
+    for y in range(Y):
+        extra[y] = parts[y, :, COLS:]
+
+
+def land_kernel(send, own, back, extra, out, grad_self, grad_neigh, grad_bias):
     out[...] = own[...]
     for slab in range(SLABS):
         for slot in range(SLOTS):
             tile = back[slab, slot * ROWS : (slot + 1) * ROWS, :].astype(F32)
             out[:, lanes(send[slot, slab])] += tile
-    for slab in range(SLABS):
-        value = back[slab, SLOTS * ROWS :, :].astype(F32)
-        for k in range(0, CHUNK, 8):
-            block, at = divmod(slab * CHUNK + k, F)
-            if block < 4:
-                target = (grad_self, grad_neigh)[block // 2]
-                lane = (block % 2) * TILE
-                target[at : at + 8, lane : lane + TILE] = value[k : k + 8]
-            elif at == 0:
-                for half in range(2):
-                    grad_bias[:, half * TILE : (half + 1) * TILE] = value[k + half : k + half + 1]
+    for y in range(Y):
+        for x in range(X):
+            at = (y * X + x) * ROWS
+            value = extra[y, :, x * 2 * H : (x + 1) * 2 * H].astype(F32)
+            grad_self[at : at + ROWS, :] = value[:, :H]
+            grad_neigh[at : at + ROWS, :] = value[:, H:]
+    each = X * PER
+    for half in range(H // TILE):
+        first = half * (TILE // each)
+        value = extra[first, :, X * 2 * H :].astype(F32)
+        for k in range(1, TILE // each):
+            value += pltpu.roll(extra[first + k, :, X * 2 * H :].astype(F32), k * each, 1)
+        grad_bias[:, half * TILE : (half + 1) * TILE] = value[:1]
 
 
 def local(
@@ -270,17 +295,19 @@
     vert, feat = ("z", "c"), ("y", "x")
     send = jnp.swapaxes(send_list[0], 0, 1)
     first = (lax.axis_index(feat) * OWNED).astype(jnp.int32).reshape(1)
-    outgoing = call(pick_kernel, [SMEM, VMEM], struct((SLABS, SLOTS * ROWS, TILE), BF))(
-        send, node_feats
-    )
+    outgoing, feats = call(
+        pick_kernel,
+        [SMEM, VMEM],
+        (struct((SLABS, SLOTS * ROWS, TILE), BF), struct((ROWS, OWN_COLS), BF)),
+    )(send, node_feats)
     incoming = lax.all_to_all(outgoing, vert, 0, 0, tiled=True)
-    table = call(table_kernel, [VMEM, VMEM], struct((ROWS, COLS), BF))(node_feats, incoming)
+    table = call(table_kernel, [VMEM, VMEM], struct((ROWS, COLS), BF))(feats, incoming)
     table = lax.all_gather(table, "x", axis=0, tiled=True)
     table = lax.all_gather(table, "y", axis=0, tiled=True)
     activated, terms, grads = call(
         layer_kernel,
         [SMEM] * 4 + [HBM] * 6,
-        (struct((OWNED, H), BF), struct((F, COLS), BF), struct((GRAD_ROWS, TILE), F32)),
+        (struct((OWNED, H), BF), struct((F, COLS), BF), struct((MEMBERS, ROWS, WIDE), F32)),
         (
             pltpu.VMEM((F, COLS), BF),
             pltpu.VMEM((F, COLS), BF),
@@ -291,6 +318,7 @@
             pltpu.VMEM((OWNED, H), BF),
             pltpu.VMEM((F + 8, OWNED), F32),
             pltpu.VMEM((F, COLS), F32),
+            pltpu.VMEM((3, F, TILE), BF),
             pltpu.SemaphoreType.DMA((1 + FETCHES + 4,)),
         ),
         (VMEM, HBM, VMEM),
@@ -308,29 +336,34 @@
         grad_out,
     )
     terms = lax.psum_scatter(terms, "x", scatter_dimension=0, tiled=True)
-    grads = grads.reshape(SLABS, CHUNK, TILE)
+    grads = lax.all_to_all(grads, feat, 0, 0, tiled=True)
+    grads = call(feat_sum_kernel, [VMEM], struct((SLABS, ROWS, WIDE), F32))(grads)
     grads = lax.all_to_all(grads, vert, 0, 0, tiled=True)
-    grads = call(spread_kernel, [VMEM], struct((MEMBERS, CHUNK, TILE), F32))(grads)
-    grads = lax.all_to_all(grads, feat, 0, 0, tiled=True)
+    grads = call(vert_sum_kernel, [VMEM], struct((ROWS, WIDE), F32))(grads)
+    grads = lax.all_gather(grads, "x", axis=0, tiled=False)
     terms, grads = lax.optimization_barrier((terms, grads))
-    terms = call(cut_kernel, [VMEM], struct((Y, ROWS, COLS), BF))(terms)
+    terms = call(join_kernel, [VMEM, VMEM], struct((Y, ROWS, COLS + EXTRA), BF))(terms, grads)
     terms = lax.all_to_all(terms, "y", 0, 0, tiled=True)
-    own, away = call(
+    own, away, extra = call(
         sum_kernel,
-        [VMEM, VMEM],
-        (struct((ROWS, OWN_COLS), F32), struct((SLABS, SLOTS * ROWS + CHUNK, TILE), BF)),
-    )(terms, grads)
+        [VMEM],
+        (
+            struct((ROWS, OWN_COLS), F32),
+            struct((SLABS, SLOTS * ROWS, TILE), BF),
+            struct((Y, ROWS, EXTRA), BF),
+        ),
+    )(terms)
     back = lax.all_to_all(away, vert, 0, 0, tiled=True)
     grad_feats, grad_self, grad_neigh, grad_bias = call(
         land_kernel,
-        [SMEM, VMEM, VMEM],
+        [SMEM, VMEM, VMEM, VMEM],
         (
             struct((ROWS, OWN_COLS), F32),
             struct((F, H), F32),
             struct((F, H), F32),
             struct((1, H), F32),
         ),
-    )(send, own, back)
+    )(send, own, back, extra)
     return activated, grad_feats, grad_self, grad_neigh, grad_bias.reshape(H)
 
 

time: 235 us -> 229 us (0.974)
  waiting for transfers between devices: 58.4 us -> 50.5 us
  blocking collectives: 140 us -> 143 us
    all_gather x0 -> x1, blocking collectives: none -> 9.03 us  [local(): grads = lax.all_gather(grads, 'x', axis=0, tiled=False)]
    reduce_scatter x1, waiting for transfers between devices: 7.85 us -> 0.01 us  [local(): terms = lax.psum_scatter(terms, 'x', scatter_dimension=0, tiled=True)]
    all_to_all x1, blocking collectives: 31.1 us -> 27.3 us  [local(): terms = lax.all_to_all(terms, 'y', 0, 0, tiled=True)]
    all_to_all x1, blocking collectives: 26.7 us -> 30.2 us  [local(): grads = lax.all_to_all(grads, vert, 0, 0, tiled=True)]
    all_to_all x1, blocking collectives: 25.8 us -> 22.5 us  [local(): back = lax.all_to_all(away, vert, 0, 0, tiled=True)]
    all_to_all x1, blocking collectives: 19 us -> 16.3 us  [local(): grads = lax.all_to_all(grads, feat, 0, 0, tiled=True)]
    unnamed x13 -> x11, local copies, waits for them, and re-layouts: 5.34 us -> 4.51 us
  transfers between devices with their start and end apart: 2 -> 2, of which waited for: 2 -> 1; matrix products, arithmetic and copies ran while one was open for 0% -> 0% of each run, Pallas kernels for 0% -> 0%
where the time goes in v3:
time: 229 us
  blocking collectives  143 us (62%)
  waiting for transfers between devices  50.5 us (22%)
  Pallas kernels  16.3 us (7%)
  between operations  14.8 us (6%)
  local copies, waits for them, and re-layouts  4.51 us (2%)
    all_gather x1, waiting for transfers between devices, local(): table = lax.all_gather(table, 'y', axis=0, tiled=True)  50.5 us
    all_to_all x1, blocking collectives, local(): grads = lax.all_to_all(grads, vert, 0, 0, tiled=True)  30.2 us
    all_to_all x1, blocking collectives, local(): terms = lax.all_to_all(terms, 'y', 0, 0, tiled=True)  27.3 us
    all_to_all x1, blocking collectives, local(): incoming = lax.all_to_all(outgoing, vert, 0, 0, tiled=True)  26.6 us
    all_to_all x1, blocking collectives, local(): back = lax.all_to_all(away, vert, 0, 0, tiled=True)  22.5 us
    all_to_all x1, blocking collectives, local(): grads = lax.all_to_all(grads, feat, 0, 0, tiled=True)  16.3 us
    pallas_call x1, Pallas kernels, local(): call(layer_kernel, [SMEM] * 4 + [HBM] * 6, (struct((OWNED, H), BF), struc...  13.7 us
    all_gather x1, blocking collectives, local(): table = lax.all_gather(table, 'x', axis=0, tiled=True)  11 us
  transfers between devices with their start and end apart: 2, of which 1 were waited for; matrix products, arithmetic and copies ran while one was open for 0% of the time, Pallas kernels for 0%

profile of v3, /device:TPU:1, one launch (start us, length us, event | category | flops | bytes accessed | tf_op | source)
XLA Modules:
  0.0 229.0 jit_solution(16104100607434260919)
XLA Ops:
  7.2 0.0 all-gather.5.cloned.1.call-start
  7.2 0.0 copy-start.1
  7.2 0.8 copy-done.1
  8.1 0.0 copy-start.2
  8.1 0.7 copy-done.2
  8.7 0.6 shard_map.137
  9.4 26.6 %all_to_all.25.incoming = bf16[24,8,128]{2,1,0:T(8,128)(2,1)S(1)} all-to-all(bf16[24,8,128]{2,1,0:T(8,128)(2,1)S(1)} %get-tuple-element.20), channel_id=1, replica_groups=mesh['z'=12,'c'=2,'y'=8,'x'=4] {'z','c'}, dimensions={0} | all-to-all | bytes 98304 | tf_op jit(solution)/shard_map/all_to_all | solution.py:303
  36.0 11.0 %all-gather.1 = bf16[4,4,14336]{2,1,0:T(4,128)(2,1)S(1)} all-gather(bf16[1,4,14336]{2,1,0:T(4,128)(2,1)S(1)} %bitcast.8), channel_id=1, replica_groups=mesh['z'=12,'c'=2,'y'=8,'x'=4] {'x'}, dimensions={0}, use_global_device_ids=true | all-gather | bytes 573440 | tf_op jit(solution)/shard_map/all_gather | solution.py:305
  46.9 0.9 reshape.24
  47.8 0.0 all-gather.5.cloned.1.call-update
  47.8 0.0 reduce-scatter.2.cloned.1.call-start
  48.5 50.5 %all-gather.5.cloned.1.call-done.table_hbm = bf16[128,14336]{1,0:T(8,128)(2,1)} async-done(((bf16[16,14336]{1,0:T(8,128)(2,1)}), bf16[128,14336]{1,0:T(8,128)(2,1)}) %all-gather.5.cloned.1.call-update) | async-done | bytes 3670032 | tf_op jit(solution)/shard_map/all_gather | solution.py:306
  99.0 13.7 %shard_map.139 = (bf16[256,256]{1,0:T(8,128)(2,1)}, bf16[128,14336]{1,0:T(8,128)(2,1)}, f32[32,4,640]{2,1,0:T(4,128)}) custom-call(s32[96]{0:T(128)} %src.1, s32[96]{0:T(128)} %dst.1, s32[1]{0:T(128)S(6)} %copy.15.count, s32[1]{0:T(128)} %bitcast.first, bf16[128,14336]{1,0:T(8,128)(2,1)} %all-gather.5.cloned.1.call-done.table_hbm, ...), custom_call_target="tpu_custom_call" | custom-call | tf_op jit(solution)/shard_map/pallas_call | solution.py:307
  112.7 0.0 copy-start.4
  112.7 0.0 reduce-scatter.2.cloned.1.call-update
  112.8 0.9 copy-done.4
  113.7 16.3 %all_to_all.26.parts = f32[32,4,640]{2,1,0:T(4,128)S(1)} all-to-all(f32[32,4,640]{2,1,0:T(4,128)S(1)} %copy-done.4), channel_id=1, replica_groups=mesh['z'=12,'c'=2,'y'=8,'x'=4] {'y','x'}, dimensions={0} | all-to-all | bytes 655360 | tf_op jit(solution)/shard_map/all_to_all | solution.py:339
  130.0 0.1 shard_map.140
  130.1 0.0 copy-start.3
  130.1 30.2 %all_to_all.27.parts = f32[24,4,640]{2,1,0:T(4,128)S(1)} all-to-all(f32[24,4,640]{2,1,0:T(4,128)S(1)} %shard_map.140), channel_id=1, replica_groups=mesh['z'=12,'c'=2,'y'=8,'x'=4] {'z','c'}, dimensions={0} | all-to-all | bytes 491520 | tf_op jit(solution)/shard_map/all_to_all | solution.py:341
  160.3 9.0 %all-gather.2.grads = f32[4,4,640]{2,1,0:T(4,128)S(1)} all-gather(f32[1,4,640]{2,1,0:T(4,128)S(1)} %bitcast.9), channel_id=2, replica_groups=mesh['z'=12,'c'=2,'y'=8,'x'=4] {'x'}, dimensions={0}, use_global_device_ids=true | all-gather | bytes 51200 | tf_op jit(solution)/shard_map/all_gather | solution.py:343
  169.3 0.0 reduce-scatter.2.cloned.1.call-done.terms
  169.3 0.0 copy-start
  169.3 1.2 copy-done
  170.5 0.2 shard_map.142
  170.7 27.3 %all_to_all.28.parts = bf16[8,4,16512]{2,1,0:T(4,128)(2,1)S(1)} all-to-all(bf16[8,4,16512]{2,1,0:T(4,128)(2,1)S(1)} %shard_map.142), channel_id=1, replica_groups=mesh['z'=12,'c'=2,'y'=8,'x'=4] {'y'}, dimensions={0} | all-to-all | bytes 2113536 | tf_op jit(solution)/shard_map/all_to_all | solution.py:346
  198.0 0.2 shard_map.143
  198.2 22.5 %all_to_all.29.back = bf16[24,8,128]{2,1,0:T(8,128)(2,1)S(1)} all-to-all(bf16[24,8,128]{2,1,0:T(8,128)(2,1)S(1)} %get-tuple-element.27), channel_id=1, replica_groups=mesh['z'=12,'c'=2,'y'=8,'x'=4] {'z','c'}, dimensions={0} | all-to-all | bytes 98304 | tf_op jit(solution)/shard_map/all_to_all | solution.py:356
  220.8 0.0 copy-done.3
  220.8 1.4 shard_map.144
  (2 shorter events, 0.1 us)
Async XLA Ops:
  7.2 91.8 %all-gather.5.cloned.1.call-start = ((), (), s32[]{:S(2)}) async-start(), calls=%async_computation.6 | async-start | bytes 4128768 | tf_op jit(solution)/shard_map/all_gather | solution.py:306
  7.2 0.8 copy-start.1
  8.1 0.7 copy-start.2
  47.8 121.5 %reduce-scatter.2.cloned.1.call-start = ((), (), s32[]{:S(2)}) async-start(), calls=%async_computation.7 | async-start | bytes 4587520 | tf_op jit(solution)/shard_map/reduce_scatter | solution.py:338
  112.7 1.0 copy-start.4
  130.1 90.7 %copy-start.3 = (s32[1,24,2]{1,2,0:T(2,128)S(1)}, s32[1,24,2]{1,2,0:T(2,128)}, u32[]{:S(2)}) copy-start(s32[1,24,2]{1,2,0:T(2,128)} %param.18) | copy-start | bytes 580
  169.3 1.2 copy-start
Sparse Core Ops, SparseCore 0:
  48.0 51.0 all-gather.4
  112.9 50.1 reduce-scatter.1

commit v4 on v3

--- a/solution.py
+++ b/solution.py
@@ -26,7 +26,6 @@
 AWAY_COLS = AWAY * TILE
 WIDE = 2 * H + TILE
 PER = H // MEMBERS
-EXTRA = X * 2 * H + TILE
 GROUP = 8
 FETCHES = 4
 FETCH = BPD // FETCHES
@@ -111,9 +110,7 @@
     sems,
 ):
     def fetch(k, source, target):
-        copy = pltpu.make_async_copy(source, target, sems.at[k])
-        copy.start()
-        return copy
+        return pltpu.make_async_copy(source, target, sems.at[k])
 
     get_table = fetch(0, table_hbm, table)
     get_adj = [
@@ -132,6 +129,8 @@
         )
     ]
 
+    get_table.start()
+    get_adj[0].start()
     row, col = iota((F, F), 0), iota((F, F), 1)
 
     x_of, y_of = (col // ROWS) % X, col // (ROWS * X)
@@ -141,6 +140,8 @@
     terms[...] = jnp.zeros_like(terms)
     ones = jnp.ones((8, GROUP * TILE), BF)
     get_table.wait()
+    for copy in get_adj[1:] + rest:
+        copy.start()
 
     def forward(g, carry):
         left, right = [], []
@@ -232,17 +233,9 @@
 def join_kernel(terms, grads, out):
     for y in range(Y):
         out[y, :, :COLS] = terms[y * ROWS : (y + 1) * ROWS, :]
-    bias = grads[0, :, 2 * H :]
-    for x in range(1, X):
-        bias += pltpu.roll(grads[x, :, 2 * H :], x * PER, 1)
-    bias = bias.astype(BF)
-    for x in range(X):
-        value = grads[x, :, : 2 * H].astype(BF)
-        at = COLS + x * 2 * H
-        for y in range(Y):
-            out[y, :, at : at + 2 * H] = value
+    value = grads[...].astype(BF)
     for y in range(Y):
-        out[y, :, COLS + X * 2 * H :] = bias
+        out[y, :, COLS:] = value
 
 
 def sum_kernel(parts, own, away, extra):
@@ -256,28 +249,30 @@
             tile = total(OWN_COLS + (slab * SLOTS + slot) * TILE, TILE)
             away[slab, slot * ROWS : (slot + 1) * ROWS, :] = tile.astype(BF)
     for y in range(Y):
-        extra[y] = parts[y, :, COLS:]
-
-
-def land_kernel(send, own, back, extra, out, grad_self, grad_neigh, grad_bias):
+        extra[y] = parts[y, :, COLS:].astype(F32)
+
+
+def land_kernel(
+    send, place, own, back, extra0, extra1, extra2, extra3, out, grad_self, grad_neigh, grad_bias, held
+):
     out[...] = own[...]
     for slab in range(SLABS):
         for slot in range(SLOTS):
             tile = back[slab, slot * ROWS : (slot + 1) * ROWS, :].astype(F32)
             out[:, lanes(send[slot, slab])] += tile
+    for shift, extra in enumerate((extra0, extra1, extra2, extra3)):
+        held[lax.rem(place[0] + (X - shift), X)] = extra[...]
+    bias = [jnp.zeros((1, TILE), F32) for _ in range(H // TILE)]
     for y in range(Y):
+        value = jnp.concatenate([held[x, y, :, : 2 * H] for x in range(X)], axis=0)
+        at = y * X * ROWS
+        grad_self[at : at + X * ROWS, :] = value[:, :H]
+        grad_neigh[at : at + X * ROWS, :] = value[:, H:]
         for x in range(X):
-            at = (y * X + x) * ROWS
-            value = extra[y, :, x * 2 * H : (x + 1) * 2 * H].astype(F32)
-            grad_self[at : at + ROWS, :] = value[:, :H]
-            grad_neigh[at : at + ROWS, :] = value[:, H:]
-    each = X * PER
+            half, lane = divmod((y * X + x) * PER, TILE)
+            bias[half] += pltpu.roll(held[x, y, :, 2 * H :], lane, 1)[:1]
     for half in range(H // TILE):
-        first = half * (TILE // each)
-        value = extra[first, :, X * 2 * H :].astype(F32)
-        for k in range(1, TILE // each):
-            value += pltpu.roll(extra[first + k, :, X * 2 * H :].astype(F32), k * each, 1)
-        grad_bias[:, half * TILE : (half + 1) * TILE] = value[:1]
+        grad_bias[:, half * TILE : (half + 1) * TILE] = bias[half]
 
 
 def local(
@@ -340,9 +335,8 @@
     grads = call(feat_sum_kernel, [VMEM], struct((SLABS, ROWS, WIDE), F32))(grads)
     grads = lax.all_to_all(grads, vert, 0, 0, tiled=True)
     grads = call(vert_sum_kernel, [VMEM], struct((ROWS, WIDE), F32))(grads)
-    grads = lax.all_gather(grads, "x", axis=0, tiled=False)
     terms, grads = lax.optimization_barrier((terms, grads))
-    terms = call(join_kernel, [VMEM, VMEM], struct((Y, ROWS, COLS + EXTRA), BF))(terms, grads)
+    terms = call(join_kernel, [VMEM, VMEM], struct((Y, ROWS, COLS + WIDE), BF))(terms, grads)
     terms = lax.all_to_all(terms, "y", 0, 0, tiled=True)
     own, away, extra = call(
         sum_kernel,
@@ -350,20 +344,25 @@
         (
             struct((ROWS, OWN_COLS), F32),
             struct((SLABS, SLOTS * ROWS, TILE), BF),
-            struct((Y, ROWS, EXTRA), BF),
+            struct((Y, ROWS, WIDE), F32),
         ),
     )(terms)
+    others = [
+        lax.ppermute(extra, "x", [(k, (k + shift) % X) for k in range(X)]) for shift in range(1, X)
+    ]
     back = lax.all_to_all(away, vert, 0, 0, tiled=True)
+    place = lax.axis_index("x").astype(jnp.int32).reshape(1)
     grad_feats, grad_self, grad_neigh, grad_bias = call(
         land_kernel,
-        [SMEM, VMEM, VMEM, VMEM],
+        [SMEM, SMEM] + [VMEM] * 6,
         (
             struct((ROWS, OWN_COLS), F32),
             struct((F, H), F32),
             struct((F, H), F32),
             struct((1, H), F32),
         ),
-    )(send, own, back, extra)
+        (pltpu.VMEM((X, Y, ROWS, WIDE), F32),),
+    )(send, place, own, back, extra, *others)
     return activated, grad_feats, grad_self, grad_neigh, grad_bias.reshape(H)
 
 

time: 229 us -> 230 us (level)
  blocking collectives: 143 us -> 117 us
  starting transfers between devices: 0.08 us -> 20.6 us
  waiting for transfers between devices: 50.5 us -> 57.5 us
    all_to_all x1 -> x0, blocking collectives: 22.5 us -> none  [local(): back = lax.all_to_all(away, vert, 0, 0, tiled=True)]
    all_to_all x0 -> x1, starting transfers between devices: none -> 12.7 us  [local(): back = lax.all_to_all(away, vert, 0, 0, tiled=True)]
    all_gather x1 -> x0, blocking collectives: 9.03 us -> none  [local(): grads = lax.all_gather(grads, 'x', axis=0, tiled=False)]
    ppermute x0 -> x3, starting transfers between devices: none -> 7.78 us  [local(): lax.ppermute(extra, 'x', [(k, (k + shift) % X) for k in range(X)])]
    ppermute x0 -> x3, waiting for transfers between devices: none -> 4.18 us  [local(): lax.ppermute(extra, 'x', [(k, (k + shift) % X) for k in range(X)])]
    all_to_all x1, blocking collectives: 27.3 us -> 31 us  [local(): terms = lax.all_to_all(terms, 'y', 0, 0, tiled=True)]
    reduce_scatter x1, waiting for transfers between devices: 0.01 us -> 2.85 us  [local(): terms = lax.psum_scatter(terms, 'x', scatter_dimension=0, tiled=True)]
    all_to_all x1, blocking collectives: 16.3 us -> 19 us  [local(): grads = lax.all_to_all(grads, feat, 0, 0, tiled=True)]
  transfers between devices with their start and end apart: 2 -> 6, of which waited for: 1 -> 4; matrix products, arithmetic and copies ran while one was open for 0% -> 0% of each run, Pallas kernels for 0% -> 0%
where the time goes in v4:
time: 230 us; the launch traced here: 229 us
  blocking collectives  117 us (51%)
  waiting for transfers between devices  57.5 us (25%)
  starting transfers between devices  20.6 us (9%)
  Pallas kernels  14.9 us (6%)
  between operations  14.8 us (6%)
  local copies, waits for them, and re-layouts  4.5 us (2%)
    all_gather x1, waiting for transfers between devices, local(): table = lax.all_gather(table, 'y', axis=0, tiled=True)  50.5 us
    all_to_all x1, blocking collectives, local(): terms = lax.all_to_all(terms, 'y', 0, 0, tiled=True)  31 us
    all_to_all x1, blocking collectives, local(): grads = lax.all_to_all(grads, vert, 0, 0, tiled=True)  29 us
    all_to_all x1, blocking collectives, local(): incoming = lax.all_to_all(outgoing, vert, 0, 0, tiled=True)  26.6 us
    all_to_all x1, blocking collectives, local(): grads = lax.all_to_all(grads, feat, 0, 0, tiled=True)  19 us
    all_to_all x1, starting transfers between devices, local(): back = lax.all_to_all(away, vert, 0, 0, tiled=True)  12.7 us
    pallas_call x1, Pallas kernels, local(): call(layer_kernel, [SMEM] * 4 + [HBM] * 6, (struct((OWNED, H), BF), struc...  11.8 us
    all_gather x1, blocking collectives, local(): table = lax.all_gather(table, 'x', axis=0, tiled=True)  11 us
  transfers between devices with their start and end apart: 6, of which 4 were waited for; matrix products, arithmetic and copies ran while one was open for 0% of the time, Pallas kernels for 0%

profile of v4, /device:TPU:1, one launch (start us, length us, event | category | flops | bytes accessed | tf_op | source)
XLA Modules:
  0.0 229.0 jit_solution(16344698355276833729)
XLA Ops:
  7.2 0.0 all-gather.3.cloned.1.call-start
  7.2 0.0 copy-start.1
  7.2 0.8 copy-done.1
  8.1 0.7 copy-done.2
  8.7 0.6 shard_map.137
  9.4 26.6 %all_to_all.25.incoming = bf16[24,8,128]{2,1,0:T(8,128)(2,1)S(1)} all-to-all(bf16[24,8,128]{2,1,0:T(8,128)(2,1)S(1)} %get-tuple-element.20), channel_id=1, replica_groups=mesh['z'=12,'c'=2,'y'=8,'x'=4] {'z','c'}, dimensions={0} | all-to-all | bytes 98304 | tf_op jit(solution)/shard_map/all_to_all | solution.py:298
  36.0 11.0 %all-gather = bf16[4,4,14336]{2,1,0:T(4,128)(2,1)S(1)} all-gather(bf16[1,4,14336]{2,1,0:T(4,128)(2,1)S(1)} %bitcast.8), channel_id=1, replica_groups=mesh['z'=12,'c'=2,'y'=8,'x'=4] {'x'}, dimensions={0}, use_global_device_ids=true | all-gather | bytes 573440 | tf_op jit(solution)/shard_map/all_gather | solution.py:300
  46.9 0.9 reshape.27
  47.8 0.0 all-gather.3.cloned.1.call-update
  47.8 0.0 reduce-scatter.2.cloned.1.call-start
  48.5 50.5 %all-gather.3.cloned.1.call-done.table_hbm = bf16[128,14336]{1,0:T(8,128)(2,1)} async-done(((bf16[16,14336]{1,0:T(8,128)(2,1)}), bf16[128,14336]{1,0:T(8,128)(2,1)}) %all-gather.3.cloned.1.call-update) | async-done | bytes 3670032 | tf_op jit(solution)/shard_map/all_gather | solution.py:301
  99.0 11.8 %shard_map.139 = (bf16[256,256]{1,0:T(8,128)(2,1)}, bf16[128,14336]{1,0:T(8,128)(2,1)}, f32[32,4,640]{2,1,0:T(4,128)}) custom-call(s32[96]{0:T(128)} %src.1, s32[96]{0:T(128)} %dst.1, s32[1]{0:T(128)S(6)} %copy.15.count, s32[1]{0:T(128)} %bitcast.first, bf16[128,14336]{1,0:T(8,128)(2,1)} %all-gather.3.cloned.1.call-done.table_hbm, ...), custom_call_target="tpu_custom_call" | custom-call | tf_op jit(solution)/shard_map/pallas_call | solution.py:302
  110.8 0.0 reduce-scatter.2.cloned.1.call-update
  110.8 0.0 copy-start.3
  110.9 0.9 copy-done.4
  111.8 19.0 %all_to_all.26.parts = f32[32,4,640]{2,1,0:T(4,128)S(1)} all-to-all(f32[32,4,640]{2,1,0:T(4,128)S(1)} %copy-done.4), channel_id=1, replica_groups=mesh['z'=12,'c'=2,'y'=8,'x'=4] {'y','x'}, dimensions={0} | all-to-all | bytes 655360 | tf_op jit(solution)/shard_map/all_to_all | solution.py:334
  130.8 0.1 shard_map.140
  130.9 29.0 %all_to_all.27.parts = f32[24,4,640]{2,1,0:T(4,128)S(1)} all-to-all(f32[24,4,640]{2,1,0:T(4,128)S(1)} %shard_map.140), channel_id=1, replica_groups=mesh['z'=12,'c'=2,'y'=8,'x'=4] {'z','c'}, dimensions={0} | all-to-all | bytes 491520 | tf_op jit(solution)/shard_map/all_to_all | solution.py:336
  159.9 2.8 %reduce-scatter.2.cloned.1.call-done.terms = bf16[32,14336]{1,0:T(8,128)(2,1)} async-done(((bf16[128,14336]{1,0:T(8,128)(2,1)}), bf16[32,14336]{1,0:T(8,128)(2,1)}) %reduce-scatter.2.cloned.1.call-update) | async-done | bytes 917520 | tf_op jit(solution)/shard_map/reduce_scatter | solution.py:333
  162.8 1.2 copy-done
  163.9 0.2 shard_map.142
  164.2 31.0 %all_to_all.28.parts = bf16[8,4,14976]{2,1,0:T(4,128)(2,1)S(1)} all-to-all(bf16[8,4,14976]{2,1,0:T(4,128)(2,1)S(1)} %shard_map.142), channel_id=1, replica_groups=mesh['z'=12,'c'=2,'y'=8,'x'=4] {'y'}, dimensions={0} | all-to-all | bytes 1916928 | tf_op jit(solution)/shard_map/all_to_all | solution.py:340
  195.2 0.7 shard_map.143
  195.9 12.7 %all-to-all-start.4 = ((bf16[24,8,128]{2,1,0:T(8,128)(2,1)}), bf16[24,8,128]{2,1,0:T(8,128)(2,1)S(1)}, u32[]{:S(2)}, u32[]{:S(2)}) async-start(bf16[24,8,128]{2,1,0:T(8,128)(2,1)} %get-tuple-element.27), calls=%async_computation.5 | async-start | bytes 98304 | tf_op jit(solution)/shard_map/all_to_all | solution.py:353
  208.7 2.5 %collective-permute-start.2 = (f32[8,4,640]{2,1,0:T(4,128)S(1)}, f32[8,4,640]{2,1,0:T(4,128)S(1)}, u32[]{:S(2)}, u32[]{:S(2)}) collective-permute-start(f32[8,4,640]{2,1,0:T(4,128)S(1)} %get-tuple-element.28.extra0), channel_id=1, source_target_pairs={{0,3},{1,0},{2,1},{3,2},{4,7},{5,4},{6,5},{7,6},{8,11},{9,8},{10,9... | collective-permute-start | bytes 245768 | tf_op jit(solution)/shard_map/ppermute | solution.py:351
  211.2 3.1 %collective-permute-start.1 = (f32[8,4,640]{2,1,0:T(4,128)S(1)}, f32[8,4,640]{2,1,0:T(4,128)S(1)}, u32[]{:S(2)}, u32[]{:S(2)}) collective-permute-start(f32[8,4,640]{2,1,0:T(4,128)S(1)} %get-tuple-element.28.extra0), channel_id=1, source_target_pairs={{0,2},{1,3},{2,0},{3,1},{4,6},{5,7},{6,4},{7,5},{8,10},{9,11},{10,... | collective-permute-start | bytes 245768 | tf_op jit(solution)/shard_map/ppermute | solution.py:351
  214.3 2.2 collective-permute-start
  216.5 0.0 collective-permute-done.2.extra3
  216.5 1.7 collective-permute-done.1.extra2
  218.2 2.5 %collective-permute-done.extra1 = f32[8,4,640]{2,1,0:T(4,128)S(1)} collective-permute-done((f32[8,4,640]{2,1,0:T(4,128)S(1)}, f32[8,4,640]{2,1,0:T(4,128)S(1)}, u32[]{:S(2)}, u32[]{:S(2)}) %collective-permute-start) | collective-permute-done | bytes 81952 | tf_op jit(solution)/shard_map/ppermute | solution.py:351
  220.7 0.0 all-to-all-done.4.back
  220.7 1.5 shard_map.144
  (6 shorter events, 0.1 us)
Async XLA Ops:
  7.2 91.9 %all-gather.3.cloned.1.call-start = ((), (), s32[]{:S(2)}) async-start(), calls=%async_computation.6 | async-start | bytes 4128768 | tf_op jit(solution)/shard_map/all_gather | solution.py:301
  7.2 0.8 copy-start.1
  8.1 0.7 copy-start.2
  47.8 114.9 %reduce-scatter.2.cloned.1.call-start = ((), (), s32[]{:S(2)}) async-start(), calls=%async_computation.7 | async-start | bytes 4587520 | tf_op jit(solution)/shard_map/reduce_scatter | solution.py:333
  110.8 1.0 copy-start.4
  110.8 109.8 %copy-start.3 = (s32[1,24,2]{1,2,0:T(2,128)S(1)}, s32[1,24,2]{1,2,0:T(2,128)}, u32[]{:S(2)}) copy-start(s32[1,24,2]{1,2,0:T(2,128)} %param.18) | copy-start | bytes 580
  162.8 1.2 copy-start
  195.9 24.7 %all-to-all-start.4 = ((bf16[24,8,128]{2,1,0:T(8,128)(2,1)}), bf16[24,8,128]{2,1,0:T(8,128)(2,1)S(1)}, u32[]{:S(2)}, u32[]{:S(2)}) async-start(bf16[24,8,128]{2,1,0:T(8,128)(2,1)} %get-tuple-element.27), calls=%async_computation.5 | async-start | bytes 98304 | tf_op jit(solution)/shard_map/all_to_all | solution.py:353
  208.7 7.8 %collective-permute-start.2 = (f32[8,4,640]{2,1,0:T(4,128)S(1)}, f32[8,4,640]{2,1,0:T(4,128)S(1)}, u32[]{:S(2)}, u32[]{:S(2)}) collective-permute-start(f32[8,4,640]{2,1,0:T(4,128)S(1)} %get-tuple-element.28.extra0), channel_id=1, source_target_pairs={{0,3},{1,0},{2,1},{3,2},{4,7},{5,4},{6,5},{7,6},{8,11},{9,8},{10,9... | collective-permute-start | bytes 245768 | tf_op jit(solution)/shard_map/ppermute | solution.py:351
  211.2 7.0 %collective-permute-start.1 = (f32[8,4,640]{2,1,0:T(4,128)S(1)}, f32[8,4,640]{2,1,0:T(4,128)S(1)}, u32[]{:S(2)}, u32[]{:S(2)}) collective-permute-start(f32[8,4,640]{2,1,0:T(4,128)S(1)} %get-tuple-element.28.extra0), channel_id=1, source_target_pairs={{0,2},{1,3},{2,0},{3,1},{4,6},{5,7},{6,4},{7,5},{8,10},{9,11},{10,... | collective-permute-start | bytes 245768 | tf_op jit(solution)/shard_map/ppermute | solution.py:351
  214.3 6.4 %collective-permute-start = (f32[8,4,640]{2,1,0:T(4,128)S(1)}, f32[8,4,640]{2,1,0:T(4,128)S(1)}, u32[]{:S(2)}, u32[]{:S(2)}) collective-permute-start(f32[8,4,640]{2,1,0:T(4,128)S(1)} %get-tuple-element.28.extra0), channel_id=1, source_target_pairs={{0,1},{1,2},{2,3},{3,0},{4,5},{5,6},{6,7},{7,4},{8,9},{9,10},{10,1... | collective-permute-start | bytes 245768 | tf_op jit(solution)/shard_map/ppermute | solution.py:351
Sparse Core Ops, SparseCore 0:
  48.0 51.0 all-gather.2
  111.0 51.7 reduce-scatter.1

commit v5 on v3

--- a/solution.py
+++ b/solution.py
@@ -24,9 +24,11 @@
 COLS = TABLE * TILE
 OWN_COLS = OWN * TILE
 AWAY_COLS = AWAY * TILE
-WIDE = 2 * H + TILE
+PART = 16
+CHUNK = 2 * PART + 8
+TOTAL = PART + 8
 PER = H // MEMBERS
-EXTRA = X * 2 * H + TILE
+EXTRA = X * PART // ROWS * TILE + TILE
 GROUP = 8
 FETCHES = 4
 FETCH = BPD // FETCHES
@@ -78,6 +80,17 @@
 
 def dot(a, b, ca, cb):
     return lax.dot_general(a, b, (((ca,), (cb,)), ((), ())), preferred_element_type=F32)
+
+
+def split(value):
+    high = value.astype(BF)
+    return high, (value - high.astype(F32)).astype(BF)
+
+
+def gather_parts(parts, count):
+    whole = sum(parts[k, : 2 * PART, :].astype(F32) for k in range(count))
+    bias = sum(parts[k, 2 * PART :, :].astype(F32) for k in range(count))
+    return whole[:PART] + whole[PART:], bias[:4] + bias[4:]
 
 
 def iota(shape, axis):
@@ -111,9 +124,7 @@
     sems,
 ):
     def fetch(k, source, target):
-        copy = pltpu.make_async_copy(source, target, sems.at[k])
-        copy.start()
-        return copy
+        return pltpu.make_async_copy(source, target, sems.at[k])
 
     get_table = fetch(0, table_hbm, table)
     get_adj = [
@@ -132,6 +143,8 @@
         )
     ]
 
+    get_table.start()
+    get_adj[0].start()
     row, col = iota((F, F), 0), iota((F, F), 1)
 
     x_of, y_of = (col // ROWS) % X, col // (ROWS * X)
@@ -141,6 +154,8 @@
     terms[...] = jnp.zeros_like(terms)
     ones = jnp.ones((8, GROUP * TILE), BF)
     get_table.wait()
+    for copy in get_adj[1:] + rest:
+        copy.start()
 
     def forward(g, carry):
         left, right = [], []
@@ -174,20 +189,26 @@
     act[...] = (pre * sig).astype(BF)
     grad_pre = (grad_out[...].astype(F32) * sig * (1.0 + pre * (1.0 - sig))).astype(BF)
 
-    for k, value in enumerate((own, mean)):
-        part = dot(value, grad_pre, 1, 0)
-        for m in range(MEMBERS):
-            grads[m, :, k * H : (k + 1) * H] = part[m * ROWS : (m + 1) * ROWS, :]
+    member = 0
+    for value in (own, mean):
+        both = split(dot(value, grad_pre, 1, 0))
+        for k in range(H // TILE):
+            for at in range(0, F, PART):
+                for half, piece in enumerate(both):
+                    grads[member, half * PART : (half + 1) * PART, :] = piece[
+                        at : at + PART, k * TILE : (k + 1) * TILE
+                    ]
+                member += 1
     part_bias = jnp.sum(grad_pre.astype(F32), axis=0, keepdims=True)
-    mine = iota((F, H), 1) // PER == iota((F, H), 0) // ROWS
+    mine = iota((MEMBERS, H), 1) // PER == iota((MEMBERS, H), 0)
     squeeze = (iota((H, TILE), 0) % PER == iota((H, TILE), 1)).astype(F32).astype(BF)
-    spread, rest_of = jnp.zeros((F, TILE), F32), part_bias
-    for _ in range(3):
-        high = rest_of.astype(BF).astype(F32)
-        rest_of = rest_of - high
-        spread += dot(jnp.where(mine, high, 0.0).astype(BF), squeeze, 1, 0)
+    high, low = (
+        dot(jnp.where(mine, value.astype(F32), 0.0).astype(BF), squeeze, 1, 0)
+        for value in split(part_bias)
+    )
+    upper = iota((8, TILE), 0) < 4
     for m in range(MEMBERS):
-        grads[m, :, 2 * H :] = spread[m * ROWS : (m + 1) * ROWS, :]
+        grads[m, 2 * PART :, :] = jnp.where(upper, high[m : m + 1], low[m : m + 1]).astype(BF)
 
     def reorder(value):
         return dot(order, value, 1, 0).astype(BF)
@@ -220,29 +241,37 @@
 
 
 def feat_sum_kernel(parts, out):
-    total = sum(parts[m] for m in range(MEMBERS))
+    whole, bias = gather_parts(parts, MEMBERS)
+    high, low = split(whole)
+    pair = [value.astype(F32) for value in split(bias)]
+    ends = jnp.concatenate(pair, axis=0).astype(BF)
     for k in range(SLABS):
-        out[k] = total
+        out[k, :PART, :] = high
+        out[k, PART : 2 * PART, :] = low
+        out[k, 2 * PART :, :] = ends
 
 
 def vert_sum_kernel(parts, out):
-    out[...] = sum(parts[k] for k in range(SLABS))
+    whole, bias = gather_parts(parts, SLABS)
+    out[:PART, :] = whole
+    out[PART:, :] = jnp.concatenate([bias, bias], axis=0)
 
 
 def join_kernel(terms, grads, out):
     for y in range(Y):
         out[y, :, :COLS] = terms[y * ROWS : (y + 1) * ROWS, :]
-    bias = grads[0, :, 2 * H :]
+    at = COLS
+    for x in range(X):
+        for k in range(0, PART, ROWS):
+            value = grads[x, k : k + ROWS, :].astype(BF)
+            for y in range(Y):
+                out[y, :, at : at + TILE] = value
+            at += TILE
+    bias = grads[0, PART : PART + ROWS, :]
     for x in range(1, X):
-        bias += pltpu.roll(grads[x, :, 2 * H :], x * PER, 1)
-    bias = bias.astype(BF)
-    for x in range(X):
-        value = grads[x, :, : 2 * H].astype(BF)
-        at = COLS + x * 2 * H
-        for y in range(Y):
-            out[y, :, at : at + 2 * H] = value
+        bias += pltpu.roll(grads[x, PART : PART + ROWS, :], x * PER, 1)
     for y in range(Y):
-        out[y, :, COLS + X * 2 * H :] = bias
+        out[y, :, at:] = bias.astype(BF)
 
 
 def sum_kernel(parts, own, away, extra):
@@ -265,18 +294,22 @@
         for slot in range(SLOTS):
             tile = back[slab, slot * ROWS : (slot + 1) * ROWS, :].astype(F32)
             out[:, lanes(send[slot, slab])] += tile
+    pieces = X * PART // ROWS
     for y in range(Y):
-        for x in range(X):
-            at = (y * X + x) * ROWS
-            value = extra[y, :, x * 2 * H : (x + 1) * 2 * H].astype(F32)
-            grad_self[at : at + ROWS, :] = value[:, :H]
-            grad_neigh[at : at + ROWS, :] = value[:, H:]
+        block, at = divmod(y * X * PART, F)
+        target = (grad_self, grad_neigh)[block // 2]
+        lane = (block % 2) * TILE
+        for k in range(0, pieces, 2):
+            value = jnp.concatenate(
+                [extra[y, :, j * TILE : (j + 1) * TILE].astype(F32) for j in (k, k + 1)], axis=0
+            )
+            target[at + k * ROWS : at + (k + 2) * ROWS, lane : lane + TILE] = value
     each = X * PER
     for half in range(H // TILE):
         first = half * (TILE // each)
-        value = extra[first, :, X * 2 * H :].astype(F32)
+        value = extra[first, :, pieces * TILE :].astype(F32)
         for k in range(1, TILE // each):
-            value += pltpu.roll(extra[first + k, :, X * 2 * H :].astype(F32), k * each, 1)
+            value += pltpu.roll(extra[first + k, :, pieces * TILE :].astype(F32), k * each, 1)
         grad_bias[:, half * TILE : (half + 1) * TILE] = value[:1]
 
 
@@ -307,7 +340,7 @@
     activated, terms, grads = call(
         layer_kernel,
         [SMEM] * 4 + [HBM] * 6,
-        (struct((OWNED, H), BF), struct((F, COLS), BF), struct((MEMBERS, ROWS, WIDE), F32)),
+        (struct((OWNED, H), BF), struct((F, COLS), BF), struct((MEMBERS, CHUNK, TILE), BF)),
         (
             pltpu.VMEM((F, COLS), BF),
             pltpu.VMEM((F, COLS), BF),
@@ -337,9 +370,9 @@
     )
     terms = lax.psum_scatter(terms, "x", scatter_dimension=0, tiled=True)
     grads = lax.all_to_all(grads, feat, 0, 0, tiled=True)
-    grads = call(feat_sum_kernel, [VMEM], struct((SLABS, ROWS, WIDE), F32))(grads)
+    grads = call(feat_sum_kernel, [VMEM], struct((SLABS, CHUNK, TILE), BF))(grads)
     grads = lax.all_to_all(grads, vert, 0, 0, tiled=True)
-    grads = call(vert_sum_kernel, [VMEM], struct((ROWS, WIDE), F32))(grads)
+    grads = call(vert_sum_kernel, [VMEM], struct((TOTAL, TILE), F32))(grads)
     grads = lax.all_gather(grads, "x", axis=0, tiled=False)
     terms, grads = lax.optimization_barrier((terms, grads))
     terms = call(join_kernel, [VMEM, VMEM], struct((Y, ROWS, COLS + EXTRA), BF))(terms, grads)

time: 229 us -> 230 us (level)
    all_to_all x1, blocking collectives: 30.2 us -> 27 us  [local(): grads = lax.all_to_all(grads, vert, 0, 0, tiled=True)]
    all_to_all x1, blocking collectives: 16.3 us -> 19.3 us  [local(): grads = lax.all_to_all(grads, feat, 0, 0, tiled=True)]
where the time goes in v5:
time: 230 us; the launch traced here: 229 us
  blocking collectives  143 us (62%)
  waiting for transfers between devices  50.5 us (22%)
  Pallas kernels  16.3 us (7%)
  between operations  14.7 us (6%)
  local copies, waits for them, and re-layouts  4.51 us (2%)
    all_gather x1, waiting for transfers between devices, local(): table = lax.all_gather(table, 'y', axis=0, tiled=True)  50.5 us
    all_to_all x1, blocking collectives, local(): terms = lax.all_to_all(terms, 'y', 0, 0, tiled=True)  27.3 us
    all_to_all x1, blocking collectives, local(): grads = lax.all_to_all(grads, vert, 0, 0, tiled=True)  27 us
    all_to_all x1, blocking collectives, local(): incoming = lax.all_to_all(outgoing, vert, 0, 0, tiled=True)  26.6 us
    all_to_all x1, blocking collectives, local(): back = lax.all_to_all(away, vert, 0, 0, tiled=True)  22.6 us
    all_to_all x1, blocking collectives, local(): grads = lax.all_to_all(grads, feat, 0, 0, tiled=True)  19.3 us
    pallas_call x1, Pallas kernels, local(): call(layer_kernel, [SMEM] * 4 + [HBM] * 6, (struct((OWNED, H), BF), struc...  13.7 us
    all_gather x1, blocking collectives, local(): table = lax.all_gather(table, 'x', axis=0, tiled=True)  11 us
  transfers between devices with their start and end apart: 2, of which 1 were waited for; matrix products, arithmetic and copies ran while one was open for 0% of the time, Pallas kernels for 0%

profile of v5, /device:TPU:1, one launch (start us, length us, event | category | flops | bytes accessed | tf_op | source)
XLA Modules:
  0.0 229.0 jit_solution(13095714386898100396)
XLA Ops:
  7.2 0.0 all-gather.4.cloned.1.call-start
  7.2 0.0 copy-start.1
  7.2 0.8 copy-done.1
  8.1 0.0 copy-start.2
  8.1 0.7 copy-done.2
  8.7 0.6 shard_map.137
  9.4 26.6 %all_to_all.25.incoming = bf16[24,8,128]{2,1,0:T(8,128)(2,1)S(1)} all-to-all(bf16[24,8,128]{2,1,0:T(8,128)(2,1)S(1)} %get-tuple-element.20), channel_id=1, replica_groups=mesh['z'=12,'c'=2,'y'=8,'x'=4] {'z','c'}, dimensions={0} | all-to-all | bytes 98304 | tf_op jit(solution)/shard_map/all_to_all | solution.py:336
  36.0 11.0 %all-gather.1 = bf16[4,4,14336]{2,1,0:T(4,128)(2,1)S(1)} all-gather(bf16[1,4,14336]{2,1,0:T(4,128)(2,1)S(1)} %bitcast.8), channel_id=1, replica_groups=mesh['z'=12,'c'=2,'y'=8,'x'=4] {'x'}, dimensions={0}, use_global_device_ids=true | all-gather | bytes 573440 | tf_op jit(solution)/shard_map/all_gather | solution.py:338
  46.9 0.9 reshape.24
  47.8 0.0 all-gather.4.cloned.1.call-update
  47.8 0.0 reduce-scatter.2.cloned.1.call-start
  48.5 50.5 %all-gather.4.cloned.1.call-done.table_hbm = bf16[128,14336]{1,0:T(8,128)(2,1)} async-done(((bf16[16,14336]{1,0:T(8,128)(2,1)}), bf16[128,14336]{1,0:T(8,128)(2,1)}) %all-gather.4.cloned.1.call-update) | async-done | bytes 3670032 | tf_op jit(solution)/shard_map/all_gather | solution.py:339
  99.0 13.7 %shard_map.139 = (bf16[256,256]{1,0:T(8,128)(2,1)}, bf16[128,14336]{1,0:T(8,128)(2,1)}, bf16[32,40,128]{2,1,0:T(8,128)(2,1)}) custom-call(s32[96]{0:T(128)} %src.1, s32[96]{0:T(128)} %dst.1, s32[1]{0:T(128)S(6)} %copy.15.count, s32[1]{0:T(128)} %bitcast.first, bf16[128,14336]{1,0:T(8,128)(2,1)} %all-gather.4.cloned.1.call-done.table_hbm, ...), custom_call_target="tpu_custom_call" | custom-call | tf_op jit(solution)/shard_map/pallas_call | solution.py:340
  112.7 0.0 copy-start.4
  112.7 0.0 reduce-scatter.2.cloned.1.call-update
  112.8 0.9 copy-done.4
  113.7 19.3 %all_to_all.26.parts = bf16[32,40,128]{2,1,0:T(8,128)(2,1)S(1)} all-to-all(bf16[32,40,128]{2,1,0:T(8,128)(2,1)S(1)} %copy-done.4), channel_id=1, replica_groups=mesh['z'=12,'c'=2,'y'=8,'x'=4] {'y','x'}, dimensions={0} | all-to-all | bytes 655360 | tf_op jit(solution)/shard_map/all_to_all | solution.py:372
  133.0 0.1 shard_map.140
  133.1 0.0 copy-start.3
  133.1 27.0 %all_to_all.27.parts = bf16[24,40,128]{2,1,0:T(8,128)(2,1)S(1)} all-to-all(bf16[24,40,128]{2,1,0:T(8,128)(2,1)S(1)} %shard_map.140), channel_id=1, replica_groups=mesh['z'=12,'c'=2,'y'=8,'x'=4] {'z','c'}, dimensions={0} | all-to-all | bytes 491520 | tf_op jit(solution)/shard_map/all_to_all | solution.py:374
  160.1 0.1 shard_map.141
  160.2 9.0 %all-gather = f32[96,128]{1,0:T(8,128)S(1)} all-gather(f32[24,128]{1,0:T(8,128)S(1)} %shard_map.141), channel_id=2, replica_groups=mesh['z'=12,'c'=2,'y'=8,'x'=4] {'x'}, dimensions={0}, use_global_device_ids=true | all-gather | bytes 61440 | tf_op jit(solution)/shard_map/all_gather | solution.py:376
  169.2 0.0 reduce-scatter.2.cloned.1.call-done.terms
  169.2 0.0 copy-start
  169.2 1.2 copy-done
  170.4 0.3 shard_map.142
  170.7 27.3 %all_to_all.28.parts = bf16[8,4,16512]{2,1,0:T(4,128)(2,1)S(1)} all-to-all(bf16[8,4,16512]{2,1,0:T(4,128)(2,1)S(1)} %shard_map.142), channel_id=1, replica_groups=mesh['z'=12,'c'=2,'y'=8,'x'=4] {'y'}, dimensions={0} | all-to-all | bytes 2113536 | tf_op jit(solution)/shard_map/all_to_all | solution.py:379
  198.0 0.2 shard_map.143
  198.1 22.6 %all_to_all.29.back = bf16[24,8,128]{2,1,0:T(8,128)(2,1)S(1)} all-to-all(bf16[24,8,128]{2,1,0:T(8,128)(2,1)S(1)} %get-tuple-element.27), channel_id=1, replica_groups=mesh['z'=12,'c'=2,'y'=8,'x'=4] {'z','c'}, dimensions={0} | all-to-all | bytes 98304 | tf_op jit(solution)/shard_map/all_to_all | solution.py:389
  220.8 0.0 copy-done.3
  220.8 1.4 shard_map.144
  (1 shorter events, 0.0 us)
Async XLA Ops:
  7.2 91.8 %all-gather.4.cloned.1.call-start = ((), (), s32[]{:S(2)}) async-start(), calls=%async_computation.6 | async-start | bytes 4128768 | tf_op jit(solution)/shard_map/all_gather | solution.py:339
  7.2 0.8 copy-start.1
  8.1 0.7 copy-start.2
  47.8 121.4 %reduce-scatter.2.cloned.1.call-start = ((), (), s32[]{:S(2)}) async-start(), calls=%async_computation.7 | async-start | bytes 4587520 | tf_op jit(solution)/shard_map/reduce_scatter | solution.py:371
  112.7 1.0 copy-start.4
  133.1 87.7 %copy-start.3 = (s32[1,24,2]{1,2,0:T(2,128)S(1)}, s32[1,24,2]{1,2,0:T(2,128)}, u32[]{:S(2)}) copy-start(s32[1,24,2]{1,2,0:T(2,128)} %param.18) | copy-start | bytes 580
  169.2 1.2 copy-start
Sparse Core Ops, SparseCore 0:
  48.0 51.0 all-gather.3
  112.9 50.2 reduce-scatter.1

commit v6 on v5

--- a/solution.py
+++ b/solution.py
@@ -26,10 +26,9 @@
 AWAY_COLS = AWAY * TILE
 PART = 16
 CHUNK = 2 * PART + 8
-TOTAL = PART + 8
+TOTAL = 72
 PER = H // MEMBERS
-EXTRA = X * PART // ROWS * TILE + TILE
-GROUP = 8
+GROUP = 24
 FETCHES = 4
 FETCH = BPD // FETCHES
 PIECE = COLS // 7
@@ -254,27 +253,16 @@
 def vert_sum_kernel(parts, out):
     whole, bias = gather_parts(parts, SLABS)
     out[:PART, :] = whole
-    out[PART:, :] = jnp.concatenate([bias, bias], axis=0)
-
-
-def join_kernel(terms, grads, out):
+    out[PART : PART + 8, :] = jnp.concatenate([bias, bias], axis=0)
+    out[PART + 8 :, :] = jnp.zeros((TOTAL - PART - 8, TILE), F32)
+
+
+def cut_kernel(terms, out):
     for y in range(Y):
-        out[y, :, :COLS] = terms[y * ROWS : (y + 1) * ROWS, :]
-    at = COLS
-    for x in range(X):
-        for k in range(0, PART, ROWS):
-            value = grads[x, k : k + ROWS, :].astype(BF)
-            for y in range(Y):
-                out[y, :, at : at + TILE] = value
-            at += TILE
-    bias = grads[0, PART : PART + ROWS, :]
-    for x in range(1, X):
-        bias += pltpu.roll(grads[x, PART : PART + ROWS, :], x * PER, 1)
-    for y in range(Y):
-        out[y, :, at:] = bias.astype(BF)
-
-
-def sum_kernel(parts, own, away, extra):
+        out[y] = terms[y * ROWS : (y + 1) * ROWS, :]
+
+
+def sum_kernel(parts, own, away):
     def total(at, width):
         return sum(parts[y, :, at : at + width].astype(F32) for y in range(Y))
 
@@ -284,33 +272,27 @@
         for slot in range(SLOTS):
             tile = total(OWN_COLS + (slab * SLOTS + slot) * TILE, TILE)
             away[slab, slot * ROWS : (slot + 1) * ROWS, :] = tile.astype(BF)
-    for y in range(Y):
-        extra[y] = parts[y, :, COLS:]
-
-
-def land_kernel(send, own, back, extra, out, grad_self, grad_neigh, grad_bias):
+
+
+def land_kernel(send, own, back, out):
     out[...] = own[...]
     for slab in range(SLABS):
         for slot in range(SLOTS):
             tile = back[slab, slot * ROWS : (slot + 1) * ROWS, :].astype(F32)
             out[:, lanes(send[slot, slab])] += tile
-    pieces = X * PART // ROWS
-    for y in range(Y):
-        block, at = divmod(y * X * PART, F)
+
+
+def unpack_kernel(parts, grad_self, grad_neigh, grad_bias):
+    bias = [jnp.zeros((1, TILE), F32) for _ in range(H // TILE)]
+    for m in range(MEMBERS):
+        block, at = divmod(m * PART, F)
         target = (grad_self, grad_neigh)[block // 2]
         lane = (block % 2) * TILE
-        for k in range(0, pieces, 2):
-            value = jnp.concatenate(
-                [extra[y, :, j * TILE : (j + 1) * TILE].astype(F32) for j in (k, k + 1)], axis=0
-            )
-            target[at + k * ROWS : at + (k + 2) * ROWS, lane : lane + TILE] = value
-    each = X * PER
+        target[at : at + PART, lane : lane + TILE] = parts[m, :PART, :]
+        half, lane = divmod(m * PER, TILE)
+        bias[half] += pltpu.roll(parts[m, PART : PART + 8, :], lane, 1)[:1]
     for half in range(H // TILE):
-        first = half * (TILE // each)
-        value = extra[first, :, pieces * TILE :].astype(F32)
-        for k in range(1, TILE // each):
-            value += pltpu.roll(extra[first + k, :, pieces * TILE :].astype(F32), k * each, 1)
-        grad_bias[:, half * TILE : (half + 1) * TILE] = value[:1]
+        grad_bias[:, half * TILE : (half + 1) * TILE] = bias[half]
 
 
 def local(
@@ -373,30 +355,24 @@
     grads = call(feat_sum_kernel, [VMEM], struct((SLABS, CHUNK, TILE), BF))(grads)
     grads = lax.all_to_all(grads, vert, 0, 0, tiled=True)
     grads = call(vert_sum_kernel, [VMEM], struct((TOTAL, TILE), F32))(grads)
-    grads = lax.all_gather(grads, "x", axis=0, tiled=False)
     terms, grads = lax.optimization_barrier((terms, grads))
-    terms = call(join_kernel, [VMEM, VMEM], struct((Y, ROWS, COLS + EXTRA), BF))(terms, grads)
+    grads = lax.all_gather(grads, feat, axis=0, tiled=False)
+    terms = call(cut_kernel, [VMEM], struct((Y, ROWS, COLS), BF))(terms)
     terms = lax.all_to_all(terms, "y", 0, 0, tiled=True)
-    own, away, extra = call(
+    own, away = call(
         sum_kernel,
         [VMEM],
-        (
-            struct((ROWS, OWN_COLS), F32),
-            struct((SLABS, SLOTS * ROWS, TILE), BF),
-            struct((Y, ROWS, EXTRA), BF),
-        ),
+        (struct((ROWS, OWN_COLS), F32), struct((SLABS, SLOTS * ROWS, TILE), BF)),
     )(terms)
     back = lax.all_to_all(away, vert, 0, 0, tiled=True)
-    grad_feats, grad_self, grad_neigh, grad_bias = call(
-        land_kernel,
-        [SMEM, VMEM, VMEM, VMEM],
-        (
-            struct((ROWS, OWN_COLS), F32),
-            struct((F, H), F32),
-            struct((F, H), F32),
-            struct((1, H), F32),
-        ),
-    )(send, own, back, extra)
+    grad_feats = call(land_kernel, [SMEM, VMEM, VMEM], struct((ROWS, OWN_COLS), F32))(
+        send, own, back
+    )
+    grad_self, grad_neigh, grad_bias = call(
+        unpack_kernel,
+        [VMEM],
+        (struct((F, H), F32), struct((F, H), F32), struct((1, H), F32)),
+    )(grads)
     return activated, grad_feats, grad_self, grad_neigh, grad_bias.reshape(H)
 
 

time: 230 us -> 260 us (1.13)
  waiting for transfers between devices: 50.5 us -> 83.4 us
  blocking collectives: 143 us -> 137 us
    all_gather x0 -> x1, waiting for transfers between devices: none -> 30.8 us  [local(): grads = lax.all_gather(grads, feat, axis=0, tiled=False)]
    all_gather x1 -> x0, blocking collectives: 9.02 us -> none  [local(): grads = lax.all_gather(grads, 'x', axis=0, tiled=False)]
    all_to_all x1, blocking collectives: 27.3 us -> 30.7 us  [local(): terms = lax.all_to_all(terms, 'y', 0, 0, tiled=True)]
    unnamed x11 -> x13, local copies, waits for them, and re-layouts: 4.51 us -> 5.72 us
  transfers between devices with their start and end apart: 2 -> 3, of which waited for: 1 -> 3; matrix products, arithmetic and copies ran while one was open for 0% -> 0% of each run, Pallas kernels for 0% -> 1%
where the time goes in v6:
time: 260 us; the launch traced here: 256 us
  blocking collectives  137 us (53%)
  waiting for transfers between devices  83.4 us (32%)
  Pallas kernels  15.5 us (6%)
  between operations  14.5 us (6%)
  local copies, waits for them, and re-layouts  5.72 us (2%)
    all_gather x1, waiting for transfers between devices, local(): table = lax.all_gather(table, 'y', axis=0, tiled=True)  50.5 us
    all_gather x1, waiting for transfers between devices, local(): grads = lax.all_gather(grads, feat, axis=0, tiled=False)  30.8 us
    all_to_all x1, blocking collectives, local(): terms = lax.all_to_all(terms, 'y', 0, 0, tiled=True)  30.7 us
    all_to_all x1, blocking collectives, local(): grads = lax.all_to_all(grads, vert, 0, 0, tiled=True)  27.3 us
    all_to_all x1, blocking collectives, local(): incoming = lax.all_to_all(outgoing, vert, 0, 0, tiled=True)  26.6 us
    all_to_all x1, blocking collectives, local(): back = lax.all_to_all(away, vert, 0, 0, tiled=True)  22.4 us
    all_to_all x1, blocking collectives, local(): grads = lax.all_to_all(grads, feat, 0, 0, tiled=True)  19.3 us
    pallas_call x1, Pallas kernels, local(): call(layer_kernel, [SMEM] * 4 + [HBM] * 6, (struct((OWNED, H), BF), struc...  11.6 us
  transfers between devices with their start and end apart: 3, of which 3 were waited for; matrix products, arithmetic and copies ran while one was open for 0% of the time, Pallas kernels for 1%

profile of v6, /device:TPU:1, one launch (start us, length us, event | category | flops | bytes accessed | tf_op | source)
XLA Modules:
  0.0 256.5 jit_solution(48774932888237171)
XLA Ops:
  7.2 0.0 all-gather.5.cloned.1.call-start
  7.2 0.0 copy-start.2
  7.2 0.8 copy-done.2
  8.1 0.7 copy-done.3
  8.7 0.6 shard_map.137
  9.4 26.6 %all_to_all.25.incoming = bf16[24,8,128]{2,1,0:T(8,128)(2,1)S(1)} all-to-all(bf16[24,8,128]{2,1,0:T(8,128)(2,1)S(1)} %get-tuple-element.18), channel_id=1, replica_groups=mesh['z'=12,'c'=2,'y'=8,'x'=4] {'z','c'}, dimensions={0} | all-to-all | bytes 98304 | tf_op jit(solution)/shard_map/all_to_all | solution.py:318
  36.0 11.0 %all-gather.1 = bf16[4,4,14336]{2,1,0:T(4,128)(2,1)S(1)} all-gather(bf16[1,4,14336]{2,1,0:T(4,128)(2,1)S(1)} %bitcast.9), channel_id=1, replica_groups=mesh['z'=12,'c'=2,'y'=8,'x'=4] {'x'}, dimensions={0}, use_global_device_ids=true | all-gather | bytes 573440 | tf_op jit(solution)/shard_map/all_gather | solution.py:320
  46.9 0.9 reshape.24
  47.8 0.0 all-gather.5.cloned.1.call-update
  47.9 0.0 reduce-scatter.2.cloned.1.call-start
  48.6 50.5 %all-gather.5.cloned.1.call-done.table_hbm = bf16[128,14336]{1,0:T(8,128)(2,1)} async-done(((bf16[16,14336]{1,0:T(8,128)(2,1)}), bf16[128,14336]{1,0:T(8,128)(2,1)}) %all-gather.5.cloned.1.call-update) | async-done | bytes 3670032 | tf_op jit(solution)/shard_map/all_gather | solution.py:321
  99.0 11.6 %shard_map.139 = (bf16[256,256]{1,0:T(8,128)(2,1)}, bf16[128,14336]{1,0:T(8,128)(2,1)}, bf16[32,40,128]{2,1,0:T(8,128)(2,1)}) custom-call(s32[96]{0:T(128)} %src.1, s32[96]{0:T(128)} %dst.1, s32[1]{0:T(128)S(6)} %copy.15.count, s32[1]{0:T(128)} %bitcast.first, bf16[128,14336]{1,0:T(8,128)(2,1)} %all-gather.5.cloned.1.call-done.table_hbm, ...), custom_call_target="tpu_custom_call" | custom-call | tf_op jit(solution)/shard_map/pallas_call | solution.py:322
  110.6 0.0 reduce-scatter.2.cloned.1.call-update
  110.7 0.0 copy-start.4
  110.7 0.0 all-gather.7.cloned.1.call-start
  110.7 0.9 copy-done.5
  111.6 19.3 %all_to_all.26.parts = bf16[32,40,128]{2,1,0:T(8,128)(2,1)S(1)} all-to-all(bf16[32,40,128]{2,1,0:T(8,128)(2,1)S(1)} %copy-done.5), channel_id=1, replica_groups=mesh['z'=12,'c'=2,'y'=8,'x'=4] {'y','x'}, dimensions={0} | all-to-all | bytes 655360 | tf_op jit(solution)/shard_map/all_to_all | solution.py:354
  130.9 0.1 shard_map.140
  131.0 27.3 %all_to_all.27.parts = bf16[24,40,128]{2,1,0:T(8,128)(2,1)S(1)} all-to-all(bf16[24,40,128]{2,1,0:T(8,128)(2,1)S(1)} %shard_map.140), channel_id=1, replica_groups=mesh['z'=12,'c'=2,'y'=8,'x'=4] {'z','c'}, dimensions={0} | all-to-all | bytes 491520 | tf_op jit(solution)/shard_map/all_to_all | solution.py:356
  158.3 0.7 shard_map.141
  159.0 2.1 reduce-scatter.2.cloned.1.call-done.terms
  161.1 0.0 all-gather.7.cloned.1.call-update
  161.1 0.0 copy-start.1
  161.1 1.2 copy-done.1
  162.3 0.2 shard_map.142
  162.5 30.7 %all_to_all.28.parts = bf16[8,4,14336]{2,1,0:T(4,128)(2,1)S(1)} all-to-all(bf16[8,4,14336]{2,1,0:T(4,128)(2,1)S(1)} %shard_map.142), channel_id=1, replica_groups=mesh['z'=12,'c'=2,'y'=8,'x'=4] {'y'}, dimensions={0} | all-to-all | bytes 1835008 | tf_op jit(solution)/shard_map/all_to_all | solution.py:361
  193.2 0.2 shard_map.143
  193.4 22.4 %all_to_all.29.back = bf16[24,8,128]{2,1,0:T(8,128)(2,1)S(1)} all-to-all(bf16[24,8,128]{2,1,0:T(8,128)(2,1)S(1)} %get-tuple-element.24), channel_id=1, replica_groups=mesh['z'=12,'c'=2,'y'=8,'x'=4] {'z','c'}, dimensions={0} | all-to-all | bytes 98304 | tf_op jit(solution)/shard_map/all_to_all | solution.py:367
  215.7 1.4 shard_map.144
  217.1 30.8 %all-gather.7.cloned.1.call-done = f32[2304,128]{1,0:T(8,128)} async-done(((f32[72,128]{1,0:T(8,128)}), f32[2304,128]{1,0:T(8,128)}) %all-gather.7.cloned.1.call-update) | async-done | bytes 1179664 | tf_op jit(solution)/shard_map/all_gather | solution.py:359
  247.9 1.3 copy-done
  249.2 0.7 shard_map.145
  (5 shorter events, 0.0 us)
Async XLA Ops:
  7.2 91.9 %all-gather.5.cloned.1.call-start = ((), (), s32[]{:S(2)}) async-start(), calls=%async_computation.6 | async-start | bytes 4128768 | tf_op jit(solution)/shard_map/all_gather | solution.py:321
  7.2 0.8 copy-start.2
  8.1 0.7 copy-start.3
  47.9 113.2 %reduce-scatter.2.cloned.1.call-start = ((), (), s32[]{:S(2)}) async-start(), calls=%async_computation.7 | async-start | bytes 4587520 | tf_op jit(solution)/shard_map/reduce_scatter | solution.py:353
  110.6 1.0 copy-start.5
  110.7 105.1 %copy-start.4 = (s32[1,24,2]{1,2,0:T(2,128)S(1)}, s32[1,24,2]{1,2,0:T(2,128)}, u32[]{:S(2)}) copy-start(s32[1,24,2]{1,2,0:T(2,128)} %param.18) | copy-start | bytes 580
  110.7 137.3 %all-gather.7.cloned.1.call-start = ((), (), s32[]{:S(2)}) async-start(), calls=%async_computation.8 | async-start | bytes 1216512 | tf_op jit(solution)/shard_map/all_gather | solution.py:359
  161.1 1.2 copy-start.1
  247.9 1.3 copy-start
Sparse Core Ops, SparseCore 0:
  48.0 51.0 all-gather.4
  110.8 50.2 reduce-scatter.1
  165.5 82.4 all-gather.6

commit v7 on v5

--- a/solution.py
+++ b/solution.py
@@ -29,7 +29,7 @@
 TOTAL = PART + 8
 PER = H // MEMBERS
 EXTRA = X * PART // ROWS * TILE + TILE
-GROUP = 8
+GROUP = 24
 FETCHES = 4
 FETCH = BPD // FETCHES
 PIECE = COLS // 7

time: 230 us -> 227 us (0.987)
  no operation moved by 1% of the time
where the time goes in v7:
time: 227 us
  blocking collectives  143 us (63%)
  waiting for transfers between devices  50.5 us (22%)
  between operations  14.7 us (6%)
  Pallas kernels  14.3 us (6%)
  local copies, waits for them, and re-layouts  4.51 us (2%)
    all_gather x1, waiting for transfers between devices, local(): table = lax.all_gather(table, 'y', axis=0, tiled=True)  50.5 us
    all_to_all x1, blocking collectives, local(): grads = lax.all_to_all(grads, vert, 0, 0, tiled=True)  27.2 us
    all_to_all x1, blocking collectives, local(): terms = lax.all_to_all(terms, 'y', 0, 0, tiled=True)  27.2 us
    all_to_all x1, blocking collectives, local(): incoming = lax.all_to_all(outgoing, vert, 0, 0, tiled=True)  26.6 us
    all_to_all x1, blocking collectives, local(): back = lax.all_to_all(away, vert, 0, 0, tiled=True)  22.5 us
    all_to_all x1, blocking collectives, local(): grads = lax.all_to_all(grads, feat, 0, 0, tiled=True)  19.4 us
    pallas_call x1, Pallas kernels, local(): call(layer_kernel, [SMEM] * 4 + [HBM] * 6, (struct((OWNED, H), BF), struc...  11.6 us
    all_gather x1, blocking collectives, local(): table = lax.all_gather(table, 'x', axis=0, tiled=True)  11 us
  transfers between devices with their start and end apart: 2, of which 1 were waited for; matrix products, arithmetic and copies ran while one was open for 0% of the time, Pallas kernels for 0%

profile of v7, /device:TPU:1, one launch (start us, length us, event | category | flops | bytes accessed | tf_op | source)
XLA Modules:
  0.0 226.9 jit_solution(9450313326888904891)
XLA Ops:
  7.2 0.0 all-gather.4.cloned.1.call-start
  7.2 0.0 copy-start.1
  7.2 0.8 copy-done.1
  8.1 0.0 copy-start.2
  8.1 0.7 copy-done.2
  8.7 0.6 shard_map.137
  9.4 26.6 %all_to_all.25.incoming = bf16[24,8,128]{2,1,0:T(8,128)(2,1)S(1)} all-to-all(bf16[24,8,128]{2,1,0:T(8,128)(2,1)S(1)} %get-tuple-element.20), channel_id=1, replica_groups=mesh['z'=12,'c'=2,'y'=8,'x'=4] {'z','c'}, dimensions={0} | all-to-all | bytes 98304 | tf_op jit(solution)/shard_map/all_to_all | solution.py:336
  36.0 11.0 %all-gather.1 = bf16[4,4,14336]{2,1,0:T(4,128)(2,1)S(1)} all-gather(bf16[1,4,14336]{2,1,0:T(4,128)(2,1)S(1)} %bitcast.8), channel_id=1, replica_groups=mesh['z'=12,'c'=2,'y'=8,'x'=4] {'x'}, dimensions={0}, use_global_device_ids=true | all-gather | bytes 573440 | tf_op jit(solution)/shard_map/all_gather | solution.py:338
  46.9 0.9 reshape.24
  47.8 0.0 all-gather.4.cloned.1.call-update
  47.8 0.0 reduce-scatter.2.cloned.1.call-start
  48.5 50.5 %all-gather.4.cloned.1.call-done.table_hbm = bf16[128,14336]{1,0:T(8,128)(2,1)} async-done(((bf16[16,14336]{1,0:T(8,128)(2,1)}), bf16[128,14336]{1,0:T(8,128)(2,1)}) %all-gather.4.cloned.1.call-update) | async-done | bytes 3670032 | tf_op jit(solution)/shard_map/all_gather | solution.py:339
  99.0 11.6 %shard_map.139 = (bf16[256,256]{1,0:T(8,128)(2,1)}, bf16[128,14336]{1,0:T(8,128)(2,1)}, bf16[32,40,128]{2,1,0:T(8,128)(2,1)}) custom-call(s32[96]{0:T(128)} %src.1, s32[96]{0:T(128)} %dst.1, s32[1]{0:T(128)S(6)} %copy.15.count, s32[1]{0:T(128)} %bitcast.first, bf16[128,14336]{1,0:T(8,128)(2,1)} %all-gather.4.cloned.1.call-done.table_hbm, ...), custom_call_target="tpu_custom_call" | custom-call | tf_op jit(solution)/shard_map/pallas_call | solution.py:340
  110.6 0.0 copy-start.4
  110.6 0.0 reduce-scatter.2.cloned.1.call-update
  110.7 0.9 copy-done.4
  111.6 19.4 %all_to_all.26.parts = bf16[32,40,128]{2,1,0:T(8,128)(2,1)S(1)} all-to-all(bf16[32,40,128]{2,1,0:T(8,128)(2,1)S(1)} %copy-done.4), channel_id=1, replica_groups=mesh['z'=12,'c'=2,'y'=8,'x'=4] {'y','x'}, dimensions={0} | all-to-all | bytes 655360 | tf_op jit(solution)/shard_map/all_to_all | solution.py:372
  131.0 0.1 shard_map.140
  131.1 0.0 copy-start.3
  131.1 27.2 %all_to_all.27.parts = bf16[24,40,128]{2,1,0:T(8,128)(2,1)S(1)} all-to-all(bf16[24,40,128]{2,1,0:T(8,128)(2,1)S(1)} %shard_map.140), channel_id=1, replica_groups=mesh['z'=12,'c'=2,'y'=8,'x'=4] {'z','c'}, dimensions={0} | all-to-all | bytes 491520 | tf_op jit(solution)/shard_map/all_to_all | solution.py:374
  158.3 0.1 shard_map.141
  158.3 9.0 %all-gather = f32[96,128]{1,0:T(8,128)S(1)} all-gather(f32[24,128]{1,0:T(8,128)S(1)} %shard_map.141), channel_id=2, replica_groups=mesh['z'=12,'c'=2,'y'=8,'x'=4] {'x'}, dimensions={0}, use_global_device_ids=true | all-gather | bytes 61440 | tf_op jit(solution)/shard_map/all_gather | solution.py:376
  167.3 0.0 reduce-scatter.2.cloned.1.call-done.terms
  167.3 0.0 copy-start
  167.3 1.2 copy-done
  168.5 0.3 shard_map.142
  168.8 27.2 %all_to_all.28.parts = bf16[8,4,16512]{2,1,0:T(4,128)(2,1)S(1)} all-to-all(bf16[8,4,16512]{2,1,0:T(4,128)(2,1)S(1)} %shard_map.142), channel_id=1, replica_groups=mesh['z'=12,'c'=2,'y'=8,'x'=4] {'y'}, dimensions={0} | all-to-all | bytes 2113536 | tf_op jit(solution)/shard_map/all_to_all | solution.py:379
  196.0 0.2 shard_map.143
  196.1 22.5 %all_to_all.29.back = bf16[24,8,128]{2,1,0:T(8,128)(2,1)S(1)} all-to-all(bf16[24,8,128]{2,1,0:T(8,128)(2,1)S(1)} %get-tuple-element.27), channel_id=1, replica_groups=mesh['z'=12,'c'=2,'y'=8,'x'=4] {'z','c'}, dimensions={0} | all-to-all | bytes 98304 | tf_op jit(solution)/shard_map/all_to_all | solution.py:389
  218.6 0.0 copy-done.3
  218.6 1.4 shard_map.144
  (1 shorter events, 0.0 us)
Async XLA Ops:
  7.2 91.8 %all-gather.4.cloned.1.call-start = ((), (), s32[]{:S(2)}) async-start(), calls=%async_computation.6 | async-start | bytes 4128768 | tf_op jit(solution)/shard_map/all_gather | solution.py:339
  7.2 0.8 copy-start.1
  8.1 0.7 copy-start.2
  47.8 119.5 %reduce-scatter.2.cloned.1.call-start = ((), (), s32[]{:S(2)}) async-start(), calls=%async_computation.7 | async-start | bytes 4587520 | tf_op jit(solution)/shard_map/reduce_scatter | solution.py:371
  110.6 1.0 copy-start.4
  131.1 87.5 %copy-start.3 = (s32[1,24,2]{1,2,0:T(2,128)S(1)}, s32[1,24,2]{1,2,0:T(2,128)}, u32[]{:S(2)}) copy-start(s32[1,24,2]{1,2,0:T(2,128)} %param.18) | copy-start | bytes 580
  167.3 1.2 copy-start
Sparse Core Ops, SparseCore 0:
  48.0 51.0 all-gather.3
  110.8 50.3 reduce-scatter.1
